TPU v7x, 32 devices: a whole 2x2x4 slice. The times are simulated.
32 devices in a mesh: dp: 8 (over z, x), tp: 4 (over y, core).
Axes of the slice: x: 2, y: 2, z: 4, core: 2. Of those that a mesh axis runs over, the one named last changes fastest.
Arguments:
- tokens: bfloat16 [8192, 768], P('dp'), may hold values from -6 to 6
- cotangent: bfloat16 [8192, 768], P('dp'), may hold values from -6 to 6
- w_qkv: bfloat16 [3, 768, 768], P(None, 'dp', 'tp'), may hold values from -0.21875 to 0.21875
- w_out: bfloat16 [768, 768], P('tp', 'dp'), may hold values from -1.75 to 1.75
- w_up: bfloat16 [768, 3072], P('dp', 'tp'), may hold values from -0.21875 to 0.21875
- w_down: bfloat16 [3072, 768], P('tp', 'dp'), may hold values from -0.109375 to 0.109375
- gains: bfloat16 [2, 768], P(None, 'dp'), may hold values from 0.099609375 to 1.8984375
- shifts: bfloat16 [4, 768], P(None, 'dp'), may hold values from -3 to 3
- b_qkv: bfloat16 [2, 12, 64], P(None, 'tp', 'dp'), may hold values from -3 to 3
- b_up: bfloat16 [24, 128], P('tp', 'dp'), may hold values from -3 to 3
- clip_lengths: int32 [16, 4], P('dp'), may hold values from 1 to 307, 512 in all within a row
Outputs:
- mixed: bfloat16 [8192, 768], P('dp')
- tokens_grad: float32 [8192, 768], P('dp')
- w_qkv_grad: float32 [3, 768, 768], P(None, 'dp', 'tp')
- w_out_grad: float32 [768, 768], P('tp', 'dp')
- w_up_grad: float32 [768, 3072], P('dp', 'tp')
- w_down_grad: float32 [3072, 768], P('tp', 'dp')
- gains_grad: float32 [2, 768], P(None, 'dp')
- shifts_grad: float32 [4, 768], P(None, 'dp')
- b_qkv_grad: float32 [2, 12, 64], P(None, 'tp', 'dp')
- b_up_grad: float32 [24, 128], P('tp', 'dp')
Inputs may be any that keep to these rules, and one draw needn't show every extreme that they name: `clip_lengths`: each row holds the lengths of the 4 clips packed in order into one block of 512 rows; they sum to 512 and the longest of each row is exactly 307.
All inputs are finite; a program needn't handle non-finite values.
Results may differ from a plain program's by a relative error of at most 0.015.
Values may be sent and summed in bfloat16 or wider, within the bound.
A program may use at most 128 MiB of HBM per device.

v0:
```python
import jax
import jax.numpy as jnp
from jax import lax
from jax.sharding import PartitionSpec as P

eps = 1e-06
masked = -1e30


def layer_norm(values, gain_vec, shift_vec):
    centred = values - jnp.mean(values, axis=-1, keepdims=True)
    spread = jnp.mean(centred * centred, axis=-1, keepdims=True)
    return centred * lax.rsqrt(spread + eps) * gain_vec + shift_vec


def gelu_exact(values):
    return jax.nn.gelu(values, approximate=False)


def segment_ids(lengths, row_count):
    clip_ends = jnp.cumsum(lengths)
    positions = jnp.arange(row_count, dtype=jnp.int32)
    return jnp.sum((positions[:, None] >= clip_ends[None, :]).astype(jnp.int32), axis=1)


def block_scores(query_blk, key_rows, query_seg, key_seg, score_scale):
    raw_scores = (
        jnp.einsum("qhd,khd->hqk", query_blk, key_rows, preferred_element_type=jnp.float32)
        * score_scale
    )
    same_clip = query_seg[:, None] == key_seg[None, :]
    return jnp.where(same_clip[None], raw_scores, masked)


def block_layout(queries):
    row_count = queries.shape[0]
    block_rows = 512
    return (row_count, block_rows, row_count // block_rows)


def attention_forward(queries, key_rows, values, segments):
    row_count, block_rows, block_count = block_layout(queries)
    head_count, head_width = (queries.shape[1], queries.shape[2])
    score_scale = head_width ** (-0.5)
    query_blocks = queries.reshape(block_count, block_rows, head_count, head_width)
    seg_blocks = segments.reshape(block_count, block_rows)

    def one_block(inputs):
        query_blk, query_seg = inputs
        scores = block_scores(query_blk, key_rows, query_seg, segments, score_scale)
        top_score = jnp.max(scores, axis=-1, keepdims=True)
        exponent = jnp.exp(scores - top_score)
        totals = jnp.sum(exponent, axis=-1, keepdims=True)
        probabilities = (exponent / totals).astype(jnp.bfloat16)
        output = jnp.einsum(
            "hqk,khd->qhd", probabilities, values, preferred_element_type=jnp.float32
        )
        return (output, (top_score + jnp.log(totals))[..., 0])

    outputs, log_totals = lax.map(one_block, (query_blocks, seg_blocks))
    return (outputs.reshape(row_count, head_count, head_width), log_totals)


def attention_backward(queries, key_rows, values, segments, log_totals, attended_grad):
    row_count, block_rows, block_count = block_layout(queries)
    head_count, head_width = (queries.shape[1], queries.shape[2])
    score_scale = head_width ** (-0.5)
    query_blocks = queries.reshape(block_count, block_rows, head_count, head_width)
    grad_blocks = attended_grad.reshape(block_count, block_rows, head_count, head_width)
    seg_blocks = segments.reshape(block_count, block_rows)

    def one_block(running, inputs):
        key_grad, value_grad = running
        query_blk, query_seg, log_total, grad_blk = inputs
        scores = block_scores(query_blk, key_rows, query_seg, segments, score_scale)
        probabilities = jnp.exp(scores - log_total[..., None])
        prob_low = probabilities.astype(jnp.bfloat16)
        prob_grad = jnp.einsum("qhd,khd->hqk", grad_blk, values, preferred_element_type=jnp.float32)
        row_dot = jnp.sum(probabilities * prob_grad, axis=-1, keepdims=True)
        score_grad = (probabilities * (prob_grad - row_dot)).astype(jnp.bfloat16)
        query_grad = (
            jnp.einsum("hqk,khd->qhd", score_grad, key_rows, preferred_element_type=jnp.float32)
            * score_scale
        )
        key_grad = (
            key_grad
            + jnp.einsum("hqk,qhd->khd", score_grad, query_blk, preferred_element_type=jnp.float32)
            * score_scale
        )
        value_grad = value_grad + jnp.einsum(
            "hqk,qhd->khd", prob_low, grad_blk, preferred_element_type=jnp.float32
        )
        return ((key_grad, value_grad), query_grad)

    empty_grad = jnp.zeros(key_rows.shape, jnp.float32)
    (key_grad, value_grad), query_grads = lax.scan(
        one_block, (empty_grad, empty_grad), (query_blocks, seg_blocks, log_totals, grad_blocks)
    )
    return (query_grads.reshape(row_count, head_count, head_width), key_grad, value_grad)


def fetch_weights(w_qkv, w_out, w_up, w_down, gains, shifts, b_qkv, b_up):
    return (
        lax.all_gather(w_qkv, "dp", axis=1, tiled=True),
        lax.all_gather(w_out, "dp", axis=1, tiled=True),
        lax.all_gather(w_up, "dp", axis=0, tiled=True),
        lax.all_gather(w_down, "dp", axis=1, tiled=True),
        lax.all_gather(gains, "dp", axis=1, tiled=True),
        lax.all_gather(shifts, "dp", axis=1, tiled=True),
        lax.all_gather(b_qkv, "dp", axis=2, tiled=True),
        lax.all_gather(b_up, "dp", axis=1, tiled=True),
    )


def reduce_grads(gradient):
    return (
        lax.psum_scatter(gradient[0], "dp", scatter_dimension=1, tiled=True),
        lax.psum_scatter(gradient[1], "dp", scatter_dimension=1, tiled=True),
        lax.psum_scatter(gradient[2], "dp", scatter_dimension=0, tiled=True),
        lax.psum_scatter(gradient[3], "dp", scatter_dimension=1, tiled=True),
        lax.psum_scatter(gradient[4], "dp", scatter_dimension=1, tiled=True),
        lax.psum_scatter(gradient[5], "dp", scatter_dimension=1, tiled=True),
        lax.psum_scatter(gradient[6], "dp", scatter_dimension=2, tiled=True),
        lax.psum_scatter(gradient[7], "dp", scatter_dimension=1, tiled=True),
    )


def micro_step(token_rows, grad_rows, lengths, gathered):
    w_qkv, w_out, w_up, w_down, gains, shifts, b_qkv, b_up = gathered
    row_count = token_rows.shape[0]
    local_heads = b_qkv.shape[1]
    head_width = b_qkv.shape[2]
    head_shape = (row_count, local_heads, head_width)
    gain_float = gains.astype(jnp.float32)
    shift_float = shifts.astype(jnp.float32)
    segments = segment_ids(lengths, row_count)
    inputs = token_rows.astype(jnp.float32)
    out_grad = grad_rows.astype(jnp.float32)
    normed, norm_pull = jax.vjp(layer_norm, inputs, gain_float[0], shift_float[0])
    normed_low = normed.astype(jnp.bfloat16)
    projected = jnp.einsum("rd,cde->cre", normed_low, w_qkv, preferred_element_type=jnp.float32)
    bias_float = b_qkv.astype(jnp.float32).reshape(2, -1)
    queries = (projected[0] + bias_float[0]).astype(jnp.bfloat16).reshape(head_shape)
    key_rows = projected[1].astype(jnp.bfloat16).reshape(head_shape)
    values = (projected[2] + bias_float[1]).astype(jnp.bfloat16).reshape(head_shape)
    attended, log_totals = attention_forward(queries, key_rows, values, segments)
    attended_low = attended.astype(jnp.bfloat16).reshape(row_count, -1)
    attention_terms = jnp.dot(attended_low, w_out, preferred_element_type=jnp.float32)
    branch = lax.psum(attention_terms.astype(jnp.bfloat16), "tp").astype(jnp.float32)
    middle = inputs + branch + shift_float[2]
    normed_two, norm_two_pull = jax.vjp(layer_norm, middle, gain_float[1], shift_float[1])
    normed_two_low = normed_two.astype(jnp.bfloat16)
    hidden = jnp.dot(normed_two_low, w_up, preferred_element_type=jnp.float32) + b_up.astype(
        jnp.float32
    ).reshape(-1)
    activated, gelu_pull = jax.vjp(gelu_exact, hidden)
    activated_low = activated.astype(jnp.bfloat16)
    down_terms = jnp.dot(activated_low, w_down, preferred_element_type=jnp.float32)
    feedforward = lax.psum(down_terms.astype(jnp.bfloat16), "tp").astype(jnp.float32)
    block_out = (middle + feedforward + shift_float[3]).astype(jnp.bfloat16)
    down_grad = jnp.einsum(
        "rf,rd->fd", activated_low, grad_rows, preferred_element_type=jnp.float32
    )
    act_grad = jnp.einsum("rd,fd->rf", grad_rows, w_down, preferred_element_type=jnp.float32)
    hidden_grad = gelu_pull(act_grad)[0].astype(jnp.bfloat16)
    up_grad = jnp.einsum(
        "rd,rf->df", normed_two_low, hidden_grad, preferred_element_type=jnp.float32
    )
    up_bias_grad = jnp.sum(hidden_grad.astype(jnp.float32), axis=0).reshape(b_up.shape)
    second_terms = jnp.einsum("rf,df->rd", hidden_grad, w_up, preferred_element_type=jnp.float32)
    normed_two_grad = lax.psum(second_terms.astype(jnp.bfloat16), "tp").astype(jnp.float32)
    middle_part, gain_two_grad, shift_two_grad = norm_two_pull(normed_two_grad)
    middle_grad = out_grad + middle_part
    middle_low = middle_grad.astype(jnp.bfloat16)
    out_proj_grad = jnp.einsum(
        "re,rd->ed", attended_low, middle_low, preferred_element_type=jnp.float32
    )
    attended_grad = (
        jnp.einsum("rd,ed->re", middle_low, w_out, preferred_element_type=jnp.float32)
        .astype(jnp.bfloat16)
        .reshape(head_shape)
    )
    query_grad, key_grad, value_grad = attention_backward(
        queries, key_rows, values, segments, log_totals, attended_grad
    )
    qkv_grad = (
        jnp.stack([query_grad, key_grad, value_grad]).astype(jnp.bfloat16).reshape(3, row_count, -1)
    )
    qkv_weight_grad = jnp.einsum(
        "rd,cre->cde", normed_low, qkv_grad, preferred_element_type=jnp.float32
    )
    qkv_bias_grad = jnp.stack(
        [
            jnp.sum(qkv_grad[0].astype(jnp.float32), axis=0),
            jnp.sum(qkv_grad[2].astype(jnp.float32), axis=0),
        ]
    ).reshape(b_qkv.shape)
    first_terms = jnp.einsum("cre,cde->rd", qkv_grad, w_qkv, preferred_element_type=jnp.float32)
    normed_grad = lax.psum(first_terms.astype(jnp.bfloat16), "tp").astype(jnp.float32)
    input_part, gain_one_grad, shift_one_grad = norm_pull(normed_grad)
    input_grad = middle_grad + input_part
    row_stats = jnp.stack(
        [gain_one_grad, gain_two_grad, shift_one_grad, shift_two_grad, jnp.sum(middle_grad, axis=0)]
    )
    gain_grad = jnp.stack([row_stats[0], row_stats[1]])
    shift_grad = jnp.stack([row_stats[2], row_stats[3], row_stats[4], jnp.sum(out_grad, axis=0)])
    weight_grads = (
        qkv_weight_grad,
        out_proj_grad,
        up_grad,
        down_grad,
        gain_grad,
        shift_grad,
        qkv_bias_grad,
        up_bias_grad,
    )
    return (block_out, input_grad, weight_grads)


def body(tokens, cotangent, w_qkv, w_out, w_up, w_down, gains, shifts, b_qkv, b_up, clip_lengths):
    batch_count = clip_lengths.shape[0]
    row_count = tokens.shape[0] // batch_count
    out_rows = []
    grad_rows = []
    shard_sum = None
    for batch_index in range(batch_count):
        start_row = batch_index * row_count
        gathered = fetch_weights(w_qkv, w_out, w_up, w_down, gains, shifts, b_qkv, b_up)
        block_out, input_grad, weight_grads = micro_step(
            tokens[start_row : start_row + row_count],
            cotangent[start_row : start_row + row_count],
            clip_lengths[batch_index],
            gathered,
        )
        out_rows.append(block_out)
        grad_rows.append(input_grad)
        shares = reduce_grads(weight_grads)
        shard_sum = shares if shard_sum is None else jax.tree.map(jnp.add, shard_sum, shares)
    return (
        jnp.concatenate(out_rows, axis=0),
        jnp.concatenate(grad_rows, axis=0),
        shard_sum[0],
        shard_sum[1],
        shard_sum[2],
        shard_sum[3],
        shard_sum[4],
        shard_sum[5],
        shard_sum[6],
        shard_sum[7],
    )


def solution(mesh):
    return jax.shard_map(
        body,
        mesh=mesh,
        in_specs=(
            P("dp", None),
            P("dp", None),
            P(None, "dp", "tp"),
            P("tp", "dp"),
            P("dp", "tp"),
            P("tp", "dp"),
            P(None, "dp"),
            P(None, "dp"),
            P(None, "tp", "dp"),
            P("tp", "dp"),
            P("dp", None),
        ),
        out_specs=(
            P("dp", None),
            P("dp", None),
            P(None, "dp", "tp"),
            P("tp", "dp"),
            P("dp", "tp"),
            P("tp", "dp"),
            P(None, "dp"),
            P(None, "dp"),
            P(None, "tp", "dp"),
            P("tp", "dp"),
        ),
        check_vma=False,
    )
```

profile of v0, /device:TPU:0, one launch (start us, length us, event | category | flops | bytes accessed | tf_op | source)
XLA Modules:
  0.0 849.7 jit_solution(56108958151637643)
XLA Ops:
  9.4 22.3 %all-gather = bf16[8,96,2]{1,2,0:T(2,128)(2,1)S(1)} all-gather(bf16[1,96,2]{1,2,0:T(2,128)(2,1)} %bitcast.213), channel_id=1, replica_groups=mesh['dp'=8,'tp'=4] {'dp'}, dimensions={0}, use_global_device_ids=true | all-gather | bytes 3456 | tf_op jit(solution)/shard_map/all_gather | solution.py:108
  32.4 2.4 fusion.26
  35.4 16.3 %all-gather.1 = bf16[8,96,4]{1,2,0:T(4,128)(2,1)S(1)} all-gather(bf16[1,96,4]{1,2,0:T(4,128)(2,1)S(1)} %bitcast.212), channel_id=1, replica_groups=mesh['dp'=8,'tp'=4] {'dp'}, dimensions={0}, use_global_device_ids=true | all-gather | bytes 6912 | tf_op jit(solution)/shard_map/all_gather | solution.py:109
  52.5 35.6 %all_gather.34 = bf16[3,768,192]{2,0,1:T(4,128)(2,1)S(1)} all-gather(bf16[3,96,192]{2,0,1:T(4,128)(2,1)S(1)} %copy.95), channel_id=1, replica_groups=mesh['dp'=8,'tp'=4] {'dp'}, dimensions={1}, use_global_device_ids=true | all-gather | bytes 995328 | tf_op jit(solution)/shard_map/all_gather | solution.py:104
  88.2 2.1 copy.96
  90.3 2.0 fusion.107
  93.3 30.4 %all_gather.35 = bf16[2,3,64]{1,0,2:T(2,128)(2,1)S(1)} all-gather(bf16[2,3,8]{1,0,2:T(2,128)(2,1)S(1)} %copy.97), channel_id=1, replica_groups=mesh['dp'=8,'tp'=4] {'dp'}, dimensions={2}, use_global_device_ids=true | all-gather | bytes 864 | tf_op jit(solution)/shard_map/all_gather | solution.py:110
  124.3 31.0 %all_gather.36 = bf16[192,768]{0,1:T(8,128)(2,1)S(1)} all-gather(bf16[192,96]{0,1:T(8,128)(2,1)S(1)} %copy.101), channel_id=1, replica_groups=mesh['dp'=8,'tp'=4] {'dp'}, dimensions={1}, use_global_device_ids=true | all-gather | bytes 331776 | tf_op jit(solution)/shard_map/all_gather | solution.py:105
  160.3 33.3 %all-reduce.8.cloned.1.call-done = bf16[512,768]{1,0:T(8,128)(2,1)} async-done(((bf16[512,768]{1,0:T(8,128)(2,1)}), bf16[512,768]{1,0:T(8,128)(2,1)}) %all-reduce.8.cloned.1.call-update) | async-done | bytes 786448 | tf_op jit(solution)/shard_map/psum | solution.py:149
  202.2 26.2 %all-gather.2 = bf16[8,16,6]{1,2,0:T(8,128)(2,1)S(1)} all-gather(bf16[1,16,6]{1,2,0:T(8,128)(2,1)S(1)} %bitcast.211), channel_id=1, replica_groups=mesh['dp'=8,'tp'=4] {'dp'}, dimensions={0}, use_global_device_ids=true | all-gather | bytes 1728 | tf_op jit(solution)/shard_map/all_gather | solution.py:111
  229.7 6.2 all-reduce.10.cloned.1.call-done
  235.9 1.9 multiply_reduce_fusion.3
  240.5 4.6 all-gather.6.cloned.1.call-done
  245.2 6.8 multiply_convert_fusion.2
  252.0 35.3 %all-gather.8.cloned.1.call-done = bf16[768,768]{0,1:T(8,128)(2,1)} async-done(((bf16[768,96]{0,1:T(8,128)(2,1)}), bf16[768,768]{0,1:T(8,128)(2,1)}) %all-gather.8.cloned.1.call-update) | async-done | bytes 1179664 | tf_op jit(solution)/shard_map/all_gather | solution.py:107
  287.3 4.3 convert_reduce_fusion.8
  291.6 1.7 convolution_convert_fusion
  293.4 5.1 multiply_convert_fusion.3
  298.6 1.8 convert_reduce_fusion.9
  301.2 1.8 convolution_convert_fusion.1
  304.4 3.3 convolution_convert_fusion.2
  309.4 35.3 %all-reduce.14.cloned.1.call-done = (bf16[512,768]{1,0:T(8,128)(2,1)}, bf16[512,768]{1,0:T(8,128)(2,1)}) async-done(((bf16[512,768]{1,0:T(8,128)(2,1)}, bf16[512,768]{1,0:T(8,128)(2,1)}), (bf16[512,768]{1,0:T(8,128)(2,1)}, bf16[512,768]{1,0:T(8,128)(2,1)})) %all-reduce.14.cloned.1.call-update) | async-done | bytes 1572880 | tf_op jit(solution)/shard_map/psum | solution.py:171
  344.8 3.4 fusion.25
  348.2 3.1 fusion.34
  351.3 2.5 fusion.117
  365.7 1.7 bitcast_convert_fusion
  372.9 1.9 fusion.90
  376.1 2.1 fusion.75
  381.7 2.2 copy.125
  384.3 54.1 %all-reduce.12.cloned.1.call-done = (bf16[512,768]{1,0:T(8,128)(2,1)}, bf16[512,768]{1,0:T(8,128)(2,1)}, bf16[512,768]{1,0:T(8,128)(2,1)}, bf16[512,768]{1,0:T(8,128)(2,1)}) async-done(((bf16[512,768]{1,0:T(8,128)(2,1)}, bf16[512,768]{1,0:T(8,128)(2,1)}, bf16[512,768]{1,0:T(8,128)(2,1)}, bf16[512,768]{1,0:T(8,128)(2,1)}), (bf16[512,768]{1,0:T(8,128)(2,1)}, bf16[512,768]{1,0:T(8,128)(2,1)}, ...) | async-done | bytes 3145744 | tf_op jit(solution)/shard_map/psum | solution.py:159
  438.5 2.6 fusion.27
  441.3 4.1 fusion.35
  452.0 3.7 add_bitcast_fusion
  455.7 4.2 copy.123
  460.0 4.7 reshape.442
  465.4 2.2 fusion.105
  467.6 2.5 convolution_add_fusion.1
  471.5 2.0 fusion.82
  473.6 2.3 convolution_add_fusion
  479.2 21.4 %all-reduce = f32[2,3,64]{2,1,0:T(4,128)S(1)} all-reduce(f32[2,3,64]{2,1,0:T(4,128)S(1)} %maximum_add_fusion.2), channel_id=16, replica_groups=mesh['dp'=8,'tp'=4] {'dp'}, use_global_device_ids=true, to_apply=%region_60.61.clone | all-reduce | flops 384 | bytes 3072
  503.0 2.8 pad_maximum_fusion.1
  505.8 2.4 add_add_fusion.5
  508.2 1.9 pad_maximum_fusion
  510.1 54.1 %reduce-scatter.27.cloned.1.call-done = f32[96,2]{1,0:T(8,128)} async-done(((f32[768,2]{1,0:T(8,128)}), f32[96,2]{1,0:T(8,128)}) %reduce-scatter.27.cloned.1.call-update) | async-done | bytes 784
  565.6 62.7 %reduce-scatter.29.cloned.1.call-done = f32[96,4]{1,0:T(8,128)} async-done(((f32[768,4]{1,0:T(8,128)}), f32[96,4]{1,0:T(8,128)}) %reduce-scatter.29.cloned.1.call-update) | async-done | bytes 1552
  629.8 68.2 %reduce-scatter.23.cloned.1.call-done = f32[96,576]{1,0:T(8,128)} async-done(((f32[768,576]{1,0:T(8,128)}), f32[96,576]{1,0:T(8,128)}) %reduce-scatter.23.cloned.1.call-update) | async-done | bytes 221200
  699.9 70.0 %reduce-scatter.19.cloned.1.call-done = f32[96,768]{1,0:T(8,128)} async-done(((f32[768,768]{1,0:T(8,128)}), f32[96,768]{1,0:T(8,128)}) %reduce-scatter.19.cloned.1.call-update) | async-done | bytes 294928 | tf_op jit(solution)/shard_map/reduce_scatter | solution.py:119
  769.9 72.0 %reduce-scatter.21.cloned.1.call-done = f32[768,96]{0,1:T(8,128)} async-done(((f32[768,768]{0,1:T(8,128)}), f32[768,96]{0,1:T(8,128)}) %reduce-scatter.21.cloned.1.call-update) | async-done | bytes 294928 | tf_op jit(solution)/shard_map/reduce_scatter | solution.py:120
  (392 shorter events, 67.1 us)
Async XLA Ops:
  8.0 27.4 %copy-start.124 = (bf16[4,96]{1,0:T(4,128)(2,1)S(1)}, bf16[4,96]{1,0:T(4,128)(2,1)}, u32[]{:S(2)}) copy-start(bf16[4,96]{1,0:T(4,128)(2,1)} %param.18) | copy-start | bytes 2308
  8.0 44.4 %copy-start.52 = (bf16[3,96,192]{2,1,0:T(8,128)(2,1)S(1)}, bf16[3,96,192]{2,1,0:T(8,128)(2,1)}, u32[]{:S(2)}) copy-start(bf16[3,96,192]{2,1,0:T(8,128)(2,1)} %param.13) | copy-start | bytes 331780
  8.0 185.6 %all-reduce.8.cloned.1.call-start = ((), (), s32[]{:S(2)}) async-start(), calls=%async_computation.7 | async-start | bytes 1572864 | tf_op jit(solution)/shard_map/psum | solution.py:149
  9.4 80.8 %copy-start.60 = (f32[512]{0:T(512)}, f32[512]{0:T(512)S(1)}, u32[]{:S(2)}) copy-start(f32[512]{0:T(512)S(1)} %broadcast_multiply_fusion.3) | copy-start | bytes 6148
  34.9 55.4 %copy-start.79 = (f32[512]{0:T(512)}, f32[512]{0:T(512)S(1)}, u32[]{:S(2)}) copy-start(f32[512]{0:T(512)S(1)} %fusion.95) | copy-start | bytes 6148
  52.4 37.8 %copy-start.116 = (f32[768]{0:T(1024)}, f32[768]{0:T(1024)S(1)}, u32[]{:S(2)}) copy-start(f32[768]{0:T(1024)S(1)} %get-tuple-element.205) | copy-start | bytes 9220
  92.3 31.6 %copy-start.71 = (bf16[192,96]{1,0:T(8,128)(2,1)S(1)}, bf16[192,96]{1,0:T(8,128)(2,1)}, u32[]{:S(2)}) copy-start(bf16[192,96]{1,0:T(8,128)(2,1)} %param.14) | copy-start | bytes 110596
  92.3 63.7 %copy-start.24 = (bf16[1,512,192]{1,2,0:T(8,128)(2,1)}, bf16[1,512,192]{1,2,0:T(8,128)(2,1)S(1)}, u32[]{:S(2)}) copy-start(bf16[1,512,192]{1,2,0:T(8,128)(2,1)S(1)} %slice.201) | copy-start | bytes 589828
  93.0 63.1 %copy-start.19 = (f32[1,512,192]{1,2,0:T(8,128)}, f32[1,512,192]{1,2,0:T(8,128)S(1)}, u32[]{:S(2)}) copy-start(f32[1,512,192]{1,2,0:T(8,128)S(1)} %get-tuple-element.233) | copy-start | bytes 1179652
  93.0 63.6 %copy-start.28 = (f32[1,512,192]{1,2,0:T(8,128)}, f32[1,512,192]{1,2,0:T(8,128)S(1)}, u32[]{:S(2)}) copy-start(f32[1,512,192]{1,2,0:T(8,128)S(1)} %get-tuple-element.232) | copy-start | bytes 1179652
  123.9 73.8 %copy-start.73 = (f32[1,3,64]{2,1,0:T(4,128)}, f32[1,3,64]{2,1,0:T(4,128)S(1)}, u32[]{:S(2)}) copy-start(f32[1,3,64]{2,1,0:T(4,128)S(1)} %copy.98) | copy-start | bytes 2308
  123.9 72.5 %copy-start.58 = (f32[1,3,64]{2,1,0:T(4,128)}, f32[1,3,64]{2,1,0:T(4,128)S(1)}, u32[]{:S(2)}) copy-start(f32[1,3,64]{2,1,0:T(4,128)S(1)} %copy.99) | copy-start | bytes 2308
  159.7 35.7 %copy-start.32 = (bf16[3,768,192]{1,2,0:T(8,128)(2,1)S(1)}, bf16[3,768,192]{1,2,0:T(8,128)(2,1)}, u32[]{:S(2)}) copy-start(bf16[3,768,192]{1,2,0:T(8,128)(2,1)} %copy.96) | copy-start | bytes 2654212
  159.7 35.7 %copy-start.117 = (f32[768]{0:T(1024)S(1)}, f32[768]{0:T(1024)}, u32[]{:S(2)}) copy-start(f32[768]{0:T(1024)} %copy-done.116) | copy-start | bytes 9220
  159.7 76.1 %all-reduce.10.cloned.1.call-start = ((), (), s32[]{:S(2)}) async-start(), calls=%async_computation.10 | async-start | bytes 1572864 | tf_op jit(solution)/shard_map/psum | solution.py:149
  159.8 36.4 %copy-start.65 = (f32[512]{0:T(512)}, f32[512]{0:T(512)S(1)}, u32[]{:S(2)}) copy-start(f32[512]{0:T(512)S(1)} %broadcast_multiply_fusion.1) | copy-start | bytes 6148
  199.6 30.1 %copy-start.39 = (bf16[3,64,512]{2,1,0:T(8,128)(2,1)}, bf16[3,64,512]{2,1,0:T(8,128)(2,1)S(1)}, u32[]{:S(2)}) copy-start(bf16[3,64,512]{2,1,0:T(8,128)(2,1)S(1)} %fusion.64) | copy-start | bytes 589828
  199.6 36.2 %copy-start.5 = (bf16[512,768]{1,0:T(8,128)(2,1)S(1)}, bf16[512,768]{1,0:T(8,128)(2,1)}, u32[]{:S(2)}) copy-start(bf16[512,768]{1,0:T(8,128)(2,1)} %all-reduce.8.cloned.1.call-done) | copy-start | bytes 2359300
  200.9 44.2 %all-gather.6.cloned.1.call-start = ((), (), s32[]{:S(2)}) async-start(), calls=%async_computation.8 | async-start | bytes 1327104 | tf_op jit(solution)/shard_map/all_gather | solution.py:106
  201.5 85.7 %all-gather.8.cloned.1.call-start = ((), (), s32[]{:S(2)}) async-start(), calls=%async_computation.9 | async-start | bytes 1327104 | tf_op jit(solution)/shard_map/all_gather | solution.py:107
  202.1 142.6 %all-reduce.14.cloned.1.call-start = ((), (), s32[]{:S(2)}) async-start(), calls=%async_computation.19 | async-start | bytes 3145728 | tf_op jit(solution)/shard_map/psum | solution.py:171
  287.3 4.3 copy-start.128
  293.4 5.2 copy-start.12
  293.4 5.1 copy-start.126
  303.0 135.4 %all-reduce.12.cloned.1.call-start = ((), (), s32[]{:S(2)}) async-start(), calls=%async_computation.18 | async-start | bytes 6291456 | tf_op jit(solution)/shard_map/psum | solution.py:159
  353.8 5.8 copy-start.10
  355.8 9.9 %copy-start.41 = (bf16[3,64,512]{2,1,0:T(8,128)(2,1)}, bf16[3,64,512]{2,1,0:T(8,128)(2,1)S(1)}, u32[]{:S(2)}) copy-start(bf16[3,64,512]{2,1,0:T(8,128)(2,1)S(1)} %get-tuple-element.253) | copy-start | bytes 589828
  358.6 7.1 copy-start.43
  359.6 6.1 copy-start.45
  361.9 5.6 copy-start.46
  369.2 108.6 %reduce-scatter.31.cloned.1.call-start = ((), (), s32[]{:S(2)}) async-start(), calls=%async_computation.17 | async-start | bytes 73728
  372.9 128.4 %reduce-scatter.25.cloned.1.call-start = ((), (), s32[]{:S(2)}) async-start(), calls=%async_computation.14 | async-start | bytes 884736
  376.1 4.4 copy-start.104
  376.1 5.0 copy-start.103
  378.2 60.2 %copy-start.66 = (f32[512]{0:T(512)S(1)}, f32[512]{0:T(512)}, u32[]{:S(2)}) copy-start(f32[512]{0:T(512)} %copy-done.65) | copy-start | bytes 6148
  384.0 180.2 %reduce-scatter.27.cloned.1.call-start = ((), (), s32[]{:S(2)}) async-start(), calls=%async_computation.15 | async-start | bytes 442368
  441.1 4.2 copy-start.75
  441.2 4.2 copy-start.77
  441.2 5.3 copy-start.105
  441.2 5.3 copy-start.106
  445.4 6.6 copy-start.42
  445.4 6.6 copy-start.44
  448.8 179.5 %reduce-scatter.29.cloned.1.call-start = ((), (), s32[]{:S(2)}) async-start(), calls=%async_computation.16 | async-start | bytes 442368
  451.9 246.1 %reduce-scatter.23.cloned.1.call-start = ((), (), s32[]{:S(2)}) async-start(), calls=%async_computation.13 | async-start | bytes 2211840
  464.7 305.2 %reduce-scatter.19.cloned.1.call-start = ((), (), s32[]{:S(2)}) async-start(), calls=%async_computation.11 | async-start | bytes 2654208 | tf_op jit(solution)/shard_map/reduce_scatter | solution.py:119
  470.1 371.8 %reduce-scatter.21.cloned.1.call-start = ((), (), s32[]{:S(2)}) async-start(), calls=%async_computation.12 | async-start | bytes 2654208 | tf_op jit(solution)/shard_map/reduce_scatter | solution.py:120
  475.9 29.8 %copy-start.108 = (f32[512]{0:T(512)S(1)}, f32[512]{0:T(512)}, u32[]{:S(2)}) copy-start(f32[512]{0:T(512)} %get-tuple-element.181) | copy-start | bytes 6148
  475.9 29.8 %copy-start.107 = (f32[512]{0:T(512)S(1)}, f32[512]{0:T(512)}, u32[]{:S(2)}) copy-start(f32[512]{0:T(512)} %get-tuple-element.186) | copy-start | bytes 6148
  (98 other events, 206.9 us)
Sparse Core Ops, SparseCore 0:
  159.9 33.7 all-reduce.7
  201.1 34.7 all-reduce.9
  303.1 41.5 all-reduce.13
  369.3 69.0 all-reduce.11
Sparse Core Ops, SparseCore 1:
  203.6 41.5 all-gather.5
  247.2 40.0 all-gather.7
  373.6 61.3 reduce-scatter.30
  438.3 61.6 reduce-scatter.24
  503.6 60.5 reduce-scatter.26
  567.8 60.5 reduce-scatter.28
  632.1 65.9 reduce-scatter.22
  702.0 67.9 reduce-scatter.18
  773.8 68.0 reduce-scatter.20
where the time goes:
time: 858 us; the launch traced here: 850 us
  waiting for transfers between devices  497 us (58%)
  blocking collectives  183 us (21%)
  matrix products  64.7 us (8%)
  local copies, waits for them, and re-layouts  45 us (5%)
  other arithmetic  40.9 us (5%)
  between operations  18 us (2%)
    unnamed x18, waiting for transfers between devices  186 us
    reduce_scatter x1, waiting for transfers between devices, reduce_grads(): lax.psum_scatter(gradient[3], 'dp', scatter_dimension=1, tiled=True)  72 us
    reduce_scatter x1, waiting for transfers between devices, reduce_grads(): lax.psum_scatter(gradient[2], 'dp', scatter_dimension=0, tiled=True)  70 us
    psum x1, waiting for transfers between devices, micro_step(): lax.psum(down_terms.astype(jnp.bfloat16), 'tp').astype(jnp.float32)  54.1 us
    psum x2, waiting for transfers between devices, micro_step(): lax.psum(attention_terms.astype(jnp.bfloat16), 'tp').astype(jnp.float32)  39.5 us
    all_gather x1, blocking collectives, fetch_weights(): lax.all_gather(w_qkv, 'dp', axis=1, tiled=True)  35.6 us
    all_gather x1, waiting for transfers between devices, fetch_weights(): lax.all_gather(w_down, 'dp', axis=1, tiled=True)  35.3 us
    psum x1, waiting for transfers between devices, micro_step(): lax.psum(second_terms.astype(jnp.bfloat16), 'tp').astype(jnp.float32)  35.3 us
  transfers between devices with their start and end apart: 13, of which 11 were waited for; matrix products, arithmetic and copies ran while one was open for 10% of the time, Pallas kernels for 0%

commit v1 on v0

v1 whole, which is shorter than its diff:
```python
import functools
import math

import jax
import jax.numpy as jnp
from jax import lax
from jax.experimental import pallas as pl
from jax.experimental.pallas import tpu as pltpu
from jax.sharding import PartitionSpec as P

MESH = pl.DeviceIdType.MESH
F32 = jnp.float32
BF16 = jnp.bfloat16
D = 768
BLK = 512
HALF = 256
PARTS = 8
PIECE = D // PARTS
eps = 1e-06
masked = -1e30


def mm(a, b, ca, cb):
    return lax.dot_general(a, b, (((ca,), (cb,)), ((), ())), preferred_element_type=F32)


def standardize(v):
    centred = v - jnp.mean(v, axis=-1, keepdims=True)
    rstd = lax.rsqrt(jnp.mean(centred * centred, axis=-1, keepdims=True) + eps)
    return centred * rstd, rstd


def norm_back(grad, gain, z, rstd):
    n = grad * gain
    return (
        n - jnp.mean(n, axis=-1, keepdims=True) - z * jnp.mean(n * z, axis=-1, keepdims=True)
    ) * rstd


def layer_kernel(inner, nb, refs):
    (tok_h, cot_h, ws, wa, wu, wd, lens) = refs[:7]
    (mixed_h, tgrad_h, gra_o, gru_o, grd_o, small_o) = refs[7:13]
    (
        tok, cot, g, gs, prm, nrm, qh, kh, vh, pr, att, mid, n2, act, dgl, hg, ml, mgr, dqkv,
        dka, dva, pb, rc, sy, ry, mxs, tgs, gr, rx, hs, rz, sg, sgc, sgx, sgz,
        lsem, zss, zrs, xss, xrs, css, crs, yss, yrs, nss, nrs, oss, ors, rxs, rxr, rzs, rzr, sms, smr,
    ) = refs[13:]
    d = lax.axis_index("dp")
    t = lax.axis_index("tp")
    z = d // 2
    x = d % 2
    c = t % 2
    xn = d + 1 - 2 * x
    sib = t + 1 - 2 * c
    yn = lax.rem(t + 2, 4)
    later = []

    def remote(src, dst, s, r, dd, tt):
        return pltpu.make_async_remote_copy(
            src_ref=src, dst_ref=dst, send_sem=s, recv_sem=r, device_id=(dd, tt), device_id_type=MESH
        )

    def launch(copy, guard=None):
        if guard is None:
            copy.start()
        else:
            pl.when(guard)(copy.start)
        later.append((copy.wait_send, guard))

    bar = pltpu.get_barrier_semaphore()
    greet = [(d, sib), (d, yn)]
    if inner:
        greet += [(xn, t)] + [(lax.rem(d + 2 * j, 8), t) for j in (1, 2, 3)]
    for who in greet:
        pl.semaphore_signal(bar, 1, device_id=who, device_id_type=MESH)
    cp_tok = pltpu.make_async_copy(tok_h, tok, lsem.at[0])
    cp_tok.start()
    cp_cot = pltpu.make_async_copy(cot_h, cot, lsem.at[1])
    cp_cot.start()
    pl.semaphore_wait(bar, len(greet))

    shards = (wa, wu, wd, ws)

    def slot(m, i):
        return gs.at[i] if m == 3 else g.at[m, i]

    def zcopy(m, side, src, i, s):
        return remote(src, slot(m, i), zss.at[m, side, s], zrs.at[m, side, s], d + 2 - 4 * side, t)

    def xcopy(m, src, i, zsrc):
        return remote(src, slot(m, i), xss.at[m, zsrc], xrs.at[m, zsrc], xn, t)

    def gather_start(m):
        launch(zcopy(m, 0, shards[m], d, 0), z < 3)
        launch(zcopy(m, 1, shards[m], d, 0), z > 0)
        launch(xcopy(m, shards[m], d, z))

    def gather_step(m, s):
        for side in (0, 1):
            i = d - 2 * s if side == 0 else d + 2 * s
            here = z >= s if side == 0 else z + s <= 3
            onward = z < 3 if side == 0 else z > 0

            @pl.when(here)
            def _():
                zcopy(m, side, slot(m, i), i, s - 1).wait_recv()

            if s < 3:
                launch(zcopy(m, side, slot(m, i), i, s), jnp.logical_and(here, onward))
            launch(xcopy(m, slot(m, i), i, i // 2), here)

    def gather_end(m):
        for k in range(4):
            i = 2 * k + 1 - x
            xcopy(m, slot(m, i), i, k).wait_recv()

    def half_rows(b, j):
        return pl.ds(pl.multiple_of(b * BLK + lax.rem(1 - c + j, 2) * HALF, HALF), HALF)

    def own_rows(b):
        return pl.ds(pl.multiple_of(b * BLK + c * HALF, HALF), HALF)

    def ccopy(st, b):
        return remote(pb.at[st, b, 0], rc.at[st, b], css.at[st, b], crs.at[st, b], d, sib)

    def ycopy(st, b):
        return remote(sy.at[st, b], ry.at[st, b], yss.at[st, b], yrs.at[st, b], d, yn)

    def sum_part(st, b, product):
        def one(j, carry):
            pb[st, b, j] = product(half_rows(b, j)).astype(BF16)

            @pl.when(j == 0)
            def _():
                ccopy(st, b).start()

            return carry

        lax.fori_loop(0, 2, one, 0)
        later.append((ccopy(st, b).wait_send, None))

    def sum_mid(st, b):
        ccopy(st, b).wait_recv()
        sy[st, b] = (pb[st, b, 1].astype(F32) + rc[st, b].astype(F32)).astype(BF16)
        launch(ycopy(st, b))

    def sum_end(st, b):
        ycopy(st, b).wait_recv()
        return sy[st, b].astype(F32) + ry[st, b].astype(F32)

    def share(buf, k, b):
        return remote(buf.at[own_rows(b)], buf.at[own_rows(b)], nss.at[k, b], nrs.at[k, b], d, sib)

    def shared(buf, k, b):
        rows = half_rows(b, 0)
        remote(buf.at[rows], buf.at[rows], nss.at[k, b], nrs.at[k, b], d, sib).wait_recv()

    lane = lax.broadcasted_iota(jnp.int32, (1, 128), 1)
    low = lane < 64

    def mat(m):
        return g[m].reshape(D, D)

    def chunks(b, n, fn):
        def one(i, carry):
            fn(pl.ds(pl.multiple_of(b * BLK + i * (BLK // n), BLK // n), BLK // n), i)
            return carry

        lax.fori_loop(0, n, one, 0)

    def first_norm(b):
        def fn(rows, i):
            zz, _ = standardize(tok[rows].astype(F32))
            nrm[rows] = (zz * prm[0:1] + prm[2:3]).astype(BF16)

        chunks(b, 4, fn)

    def project(b):
        def fn(rows, i):
            p = mm(nrm[rows], mat(0), 1, 0) + prm[6:7]
            s0, s1, s2, s3, s4 = (p[:, 128 * k : 128 * k + 128] for k in range(5))
            for ref, s in ((qh, s0), (kh, s1), (vh, s2)):
                ref[0, rows] = jnp.where(low, s, 0.0).astype(BF16)
                ref[1, rows] = jnp.where(low, 0.0, s).astype(BF16)
            qh[2, rows] = jnp.where(low, s3, 0.0).astype(BF16)
            kh[2, rows] = jnp.where(low, pltpu.roll(s3, 64, 1), 0.0).astype(BF16)
            vh[2, rows] = jnp.where(low, s4, 0.0).astype(BF16)

        chunks(b, 2, fn)

    def attend(b):
        blk = slice(b * BLK, b * BLK + BLK)
        e0 = lens[b, 0]
        e1 = e0 + lens[b, 1]
        e2 = e1 + lens[b, 2]

        def clip_of(pos):
            return (
                (pos >= e0).astype(jnp.int32)
                + (pos >= e1).astype(jnp.int32)
                + (pos >= e2).astype(jnp.int32)
            )

        def fn(rows, i):
            q_clip = clip_of(lax.broadcasted_iota(jnp.int32, (HALF, 1), 0) + i * HALF)
            k_clip = clip_of(lax.broadcasted_iota(jnp.int32, (1, BLK), 1))
            same = q_clip == k_clip
            outs = []
            for h in range(3):
                s = mm(qh[h, rows], kh[h, blk], 1, 1) * 0.125
                s = jnp.where(same, s, masked)
                e = jnp.exp(s - jnp.max(s, axis=-1, keepdims=True))
                p = (e / jnp.sum(e, axis=-1, keepdims=True)).astype(BF16)
                pr[3 * b + h, pl.ds(pl.multiple_of(i * HALF, HALF), HALF)] = p
                outs.append(mm(p, vh[h, blk], 1, 0))
            att[rows, 0:128] = pltpu.roll(outs[2], 64, 1).astype(BF16)
            att[rows, 128:256] = (outs[0] + outs[1]).astype(BF16)

        chunks(b, 2, fn)

    def out_part(b):
        sum_part(0, b, lambda rows: mm(att[rows], g[0, :, :, 512:768].reshape(D, 256), 1, 1))

    def second_norm(b):
        rows = own_rows(b)
        m = tok[rows].astype(F32) + sum_end(0, b) + prm[4:5]
        mid[b] = m
        zz, _ = standardize(m)
        n2[rows] = (zz * prm[1:2] + prm[3:4]).astype(BF16)
        launch(share(n2, 0, b))

    def up(b):
        def fn(rows, i):
            h = mm(n2[rows], mat(1), 1, 0) + prm[7:8]
            cdf = 0.5 * (1.0 + lax.erf(h * (1.0 / math.sqrt(2.0))))
            act[rows] = (h * cdf).astype(BF16)
            dgl[rows] = cdf + h * (jnp.exp(-0.5 * h * h) * (1.0 / math.sqrt(2.0 * math.pi)))

        chunks(b, 4, fn)

    def hidden_back(b):
        def fn(rows, i):
            hgr = mm(cot[rows], mat(2), 1, 0) * dgl[rows]
            low_grad = hgr.astype(BF16)
            hg[rows] = low_grad
            sg[7:8] += jnp.sum(low_grad.astype(F32), axis=0, keepdims=True)

        chunks(b, 2, fn)

    def middle_back(b):
        rows = own_rows(b)
        total = sum_end(2, b)
        zz, rstd = standardize(mid[b])
        out_grad = cot[rows].astype(F32)
        m = out_grad + norm_back(total, prm[1:2], zz, rstd)
        mgr[b] = m
        ml[rows] = m.astype(BF16)
        launch(share(ml, 1, b))
        sg[1:2] += jnp.sum(total * zz, axis=0, keepdims=True)
        sg[3:4] += jnp.sum(total, axis=0, keepdims=True)
        sg[4:5] += jnp.sum(m, axis=0, keepdims=True)
        sg[5:6] += jnp.sum(out_grad, axis=0, keepdims=True)

    def attend_back(b):
        blk = slice(b * BLK, b * BLK + BLK)
        dka[...] = jnp.zeros_like(dka)
        dva[...] = jnp.zeros_like(dva)

        def fn(rows, i):
            da = mm(ml[rows], g[0, :, :, 512:768].reshape(D, 256), 1, 0)
            d2, d01 = da[:, 0:128], da[:, 128:256]
            dos = (
                jnp.where(low, d01, 0.0).astype(BF16),
                jnp.where(low, 0.0, d01).astype(BF16),
                jnp.where(low, pltpu.roll(d2, 64, 1), 0.0).astype(BF16),
            )
            dqs = []
            for h in range(3):
                p = pr[3 * b + h, pl.ds(pl.multiple_of(i * HALF, HALF), HALF)]
                pf = p.astype(F32)
                dp = mm(dos[h], vh[h, blk], 1, 1)
                ds = (pf * (dp - jnp.sum(pf * dp, axis=-1, keepdims=True))).astype(BF16)
                dqs.append(mm(ds, kh[h, blk], 1, 0))
                dka[h] += mm(ds, qh[h, rows], 0, 0)
                dva[h] += mm(p, dos[h], 0, 0)
            dqkv[rows, 0:128] = ((dqs[0] + dqs[1]) * 0.125).astype(BF16)
            dqkv[rows, 384:512] = (dqs[2] * 0.125).astype(BF16)

        chunks(b, 2, fn)
        dqkv[blk, 128:256] = ((dka[0] + dka[1]) * 0.125).astype(BF16)
        dqkv[blk, 256:384] = (dva[0] + dva[1]).astype(BF16)
        dqkv[blk, 384:512] = (
            dqkv[blk, 384:512].astype(F32) + pltpu.roll(dka[2], 64, 1) * 0.125
        ).astype(BF16)
        dqkv[blk, 512:640] = dva[2].astype(BF16)
        sg[6:7, 0:640] += jnp.sum(dqkv[blk, 0:640].astype(F32), axis=0, keepdims=True)

    def in_part(b):
        sum_part(3, b, lambda rows: mm(dqkv[rows, 0:640], g[0, :, :, 0:640].reshape(D, 640), 1, 1))

    def out_copies(k, buf, out, b):
        mine = pltpu.make_async_copy(buf.at[b], out.at[own_rows(b)], lsem.at[2 + 2 * k + b])
        mine.start()
        later.append((mine.wait, None))
        theirs = remote(buf.at[b], out.at[own_rows(b)], oss.at[k, b], ors.at[k, b], d, sib)
        launch(theirs)
        rows = half_rows(b, 0)
        back = remote(buf.at[b], out.at[rows], oss.at[k, b], ors.at[k, b], d, sib)
        later.append((back.wait_recv, None))

    def finish_mixed(b):
        mxs[b] = (mid[b] + sum_end(1, b) + prm[5:6]).astype(BF16)
        out_copies(0, mxs, mixed_h, b)

    def finish_tokens(b):
        total = sum_end(3, b)
        zz, rstd = standardize(tok[own_rows(b)].astype(F32))
        tgs[b] = mgr[b] + norm_back(total, prm[0:1], zz, rstd)
        out_copies(1, tgs, tgrad_h, b)
        sg[0:1] += jnp.sum(total * zz, axis=0, keepdims=True)
        sg[2:3] += jnp.sum(total, axis=0, keepdims=True)

    def xred(m, k):
        return remote(gr.at[m, 2 * k + 1 - x], rx.at[m, k], rxs.at[m, k], rxr.at[m, k], xn, t)

    def zred(m, k, zd):
        return remote(
            hs.at[m, zd], rz.at[m, k - 1], rzs.at[m, k - 1], rzr.at[m, k - 1], 2 * zd + x, t
        )

    def weight_grad(m, product):
        for half in range(2):
            gr[m, 4 * half : 4 * half + 4] = (
                product(slice(384 * half, 384 * half + 384)).astype(BF16).reshape(4, PIECE, D)
            )
            if inner:
                for k in (2 * half, 2 * half + 1):
                    launch(xred(m, k))

    outs = (gra_o, gru_o, grd_o)

    def reduce_mid(m):
        if not inner:
            return
        for k in (2, 1, 3, 0):
            zd = lax.rem(z + k, 4)
            xred(m, zd).wait_recv()
            both = gr[m, 2 * zd + x].astype(F32) + rx[m, zd].astype(F32)
            if k:
                hs[m, zd] = both.astype(BF16)
                launch(zred(m, k, zd))
            else:
                outs[m][...] = both

    def reduce_end(m):
        if not inner:
            outs[m][...] = gr[m]
            return
        for k in (1, 3, 2):
            zred(m, k, lax.rem(z + k, 4)).wait_recv()
            outs[m][...] += rz[m, k - 1].astype(F32)

    def down_grad(cols):
        return mm(cot[:, cols], act[...], 0, 0)

    def up_grad(cols):
        return mm(n2[:, cols], hg[...], 0, 0)

    def in_grad(cols):
        a1 = mm(nrm[:, cols], dqkv[:, 0:640], 0, 0)
        a2 = mm(ml[:, cols], att[...], 0, 0)
        return jnp.concatenate(
            [a1[:, 0:512], a1[:, 512:640] + a2[:, 0:128], a2[:, 128:256]], axis=1
        )

    sg[...] = jnp.zeros_like(sg)
    if inner:
        gather_start(3)
        gather_start(0)
        for m in range(3):
            cp = pltpu.make_async_copy(shards[m], g.at[m, d], lsem.at[6 + m])
            cp.start()
        cp = pltpu.make_async_copy(ws, gs.at[d], lsem.at[9])
        cp.start()
        for s in (1, 2, 3):
            gather_step(3, s)
        gather_start(1)
        gather_end(3)
        for m in range(3):
            pltpu.make_async_copy(shards[m], g.at[m, d], lsem.at[6 + m]).wait()
        cp.wait()
        total = gs[0].astype(F32)
        for i in range(1, PARTS):
            total = total + gs[i].astype(F32)
        prm[...] = total
    else:
        for m in range(3):
            pltpu.make_async_copy(shards[m], g.at[m], lsem.at[6 + m]).start()
        for m in range(3):
            pltpu.make_async_copy(shards[m], g.at[m], lsem.at[6 + m]).wait()
        prm[...] = ws[...].astype(F32)

    def step(m, s):
        if inner:
            gather_step(m, s)

    step(0, 1)
    cp_tok.wait()
    cp_cot.wait()
    for b in range(nb):
        first_norm(b)
    step(0, 2)
    step(0, 3)
    if inner:
        gather_start(2)
        gather_end(0)
    pumps = [(1, 1), (1, 2), (1, 3), (2, 1), (2, 2), (2, 3)]

    def pump():
        if pumps:
            step(*pumps.pop(0))

    for b in range(nb):
        project(b)
        attend(b)
        pump()
        out_part(b)
        pump()
        sum_mid(0, b)
        pump()
    while pumps:
        pump()
    if inner:
        gather_end(1)
    for b in range(nb):
        second_norm(b)
        shared(n2, 0, b)
        up(b)
    if inner:
        gather_end(2)
    for b in range(nb):
        hidden_back(b)
        sum_part(2, b, lambda rows: mm(hg[rows], mat(1), 1, 1))
        if b > 0:
            sum_mid(2, b - 1)
    sum_mid(2, nb - 1)
    for b in range(nb):
        sum_part(1, b, lambda rows: mm(act[rows], mat(2), 1, 1))
    weight_grad(2, down_grad)
    for b in range(nb):
        sum_mid(1, b)
    weight_grad(1, up_grad)
    for b in range(nb):
        middle_back(b)
        shared(ml, 1, b)
        attend_back(b)
        in_part(b)
        if b == 0:
            reduce_mid(2)
        sum_mid(3, b)
    weight_grad(0, in_grad)
    reduce_mid(1)
    for b in range(nb):
        finish_mixed(b)
    reduce_mid(0)
    for b in range(nb):
        finish_tokens(b)
    smc = remote(sg, sgc, sms.at[0], smr.at[0], d, sib)
    smc.start()
    reduce_end(2)
    reduce_end(1)
    smc.wait()
    row = lax.broadcasted_iota(jnp.int32, (8, 1), 0)
    total = sg[...] + jnp.where(row < 6, sgc[...], 0.0)
    if inner:
        sgx[0] = total
        smx = remote(sgx.at[0], sgx.at[1], sms.at[1], smr.at[1], xn, t)
        smx.start()
        smx.wait()
        sgz[0] = sgx[0] + sgx[1]
        for k in (1, 2, 3):
            launch(remote(sgz.at[0], sgz.at[k], sms.at[1 + k], smr.at[1 + k], lax.rem(d + 2 * k, 8), t))
        reduce_end(0)
        for k in (1, 2, 3):
            remote(sgz.at[0], sgz.at[k], sms.at[1 + k], smr.at[1 + k], xn, t).wait_recv()
        small_o[...] = (sgz[0] + sgz[1]) + (sgz[2] + sgz[3])
    else:
        small_o[...] = total
        reduce_end(0)
    for wait, guard in later:
        if guard is None:
            wait()
        else:
            pl.when(guard)(wait)


def call_kernel(inner, tokens, cotangent, ws, wa, wu, wd, lens):
    rows = tokens.shape[0]
    nb = rows // BLK
    vmem = pl.BlockSpec(memory_space=pltpu.VMEM)
    anywhere = pl.BlockSpec(memory_space=pl.ANY)
    grads = (
        jax.ShapeDtypeStruct((PIECE, D), F32)
        if inner
        else jax.ShapeDtypeStruct((PARTS, PIECE, D), BF16)
    )
    dma = pltpu.SemaphoreType.DMA
    scratch = [
        pltpu.VMEM((rows, D), BF16),
        pltpu.VMEM((rows, D), BF16),
        pltpu.VMEM((3, PARTS, PIECE, D), BF16),
        pltpu.VMEM((PARTS, 16, D), BF16),
        pltpu.VMEM((16, D), F32),
        pltpu.VMEM((rows, D), BF16),
        pltpu.VMEM((3, rows, 128), BF16),
        pltpu.VMEM((3, rows, 128), BF16),
        pltpu.VMEM((3, rows, 128), BF16),
        pltpu.VMEM((3 * nb, BLK, BLK), BF16),
        pltpu.VMEM((rows, 256), BF16),
        pltpu.VMEM((nb, HALF, D), F32),
        pltpu.VMEM((rows, D), BF16),
        pltpu.VMEM((rows, D), BF16),
        pltpu.VMEM((rows, D), F32),
        pltpu.VMEM((rows, D), BF16),
        pltpu.VMEM((rows, D), BF16),
        pltpu.VMEM((nb, HALF, D), F32),
        pltpu.VMEM((rows, 640), BF16),
        pltpu.VMEM((3, BLK, 128), F32),
        pltpu.VMEM((3, BLK, 128), F32),
        pltpu.VMEM((4, nb, 2, HALF, D), BF16),
        pltpu.VMEM((4, nb, HALF, D), BF16),
        pltpu.VMEM((4, nb, HALF, D), BF16),
        pltpu.VMEM((4, nb, HALF, D), BF16),
        pltpu.VMEM((nb, HALF, D), BF16),
        pltpu.VMEM((nb, HALF, D), F32),
        pltpu.VMEM((3, PARTS, PIECE, D), BF16),
        pltpu.VMEM((3, 4, PIECE, D), BF16),
        pltpu.VMEM((3, 4, PIECE, D), BF16),
        pltpu.VMEM((3, 3, PIECE, D), BF16),
        pltpu.VMEM((8, D), F32),
        pltpu.VMEM((8, D), F32),
        pltpu.VMEM((2, 8, D), F32),
        pltpu.VMEM((4, 8, D), F32),
        dma((10,)),
        dma((4, 2, 3)),
        dma((4, 2, 3)),
        dma((4, 4)),
        dma((4, 4)),
        dma((4, nb)),
        dma((4, nb)),
        dma((4, nb)),
        dma((4, nb)),
        dma((2, nb)),
        dma((2, nb)),
        dma((2, nb)),
        dma((2, nb)),
        dma((3, 4)),
        dma((3, 4)),
        dma((3, 3)),
        dma((3, 3)),
        dma((5,)),
        dma((5,)),
    ]

    def kernel(*refs):
        layer_kernel(inner, nb, refs)

    return pl.pallas_call(
        kernel,
        out_shape=(
            jax.ShapeDtypeStruct((rows, D), BF16),
            jax.ShapeDtypeStruct((rows, D), F32),
            grads,
            grads,
            grads,
            jax.ShapeDtypeStruct((8, D), F32),
        ),
        in_specs=[anywhere, anywhere, vmem, vmem, vmem, vmem, pl.BlockSpec(memory_space=pltpu.SMEM)],
        out_specs=(anywhere, anywhere, vmem, vmem, vmem, vmem),
        scratch_shapes=scratch,
        compiler_params=pltpu.CompilerParams(
            collective_id=0, has_side_effects=True, vmem_limit_bytes=60 * 2**20
        ),
    )(tokens, cotangent, ws, wa, wu, wd, lens)


def pack_heads(q, k, v, o):
    return jnp.concatenate(
        [
            q[..., :128], k[..., :128], v[..., :128],
            q[..., 128:], k[..., 128:], v[..., 128:], o[..., 128:], o[..., :128],
        ],
        axis=-1,
    )


def unpack_heads(w):
    q = jnp.concatenate([w[..., 0:128], w[..., 384:448]], axis=-1)
    k = jnp.concatenate([w[..., 128:256], w[..., 448:512]], axis=-1)
    v = jnp.concatenate([w[..., 256:384], w[..., 512:576]], axis=-1)
    o = jnp.concatenate([w[..., 640:768], w[..., 576:640]], axis=-1)
    return q, k, v, o


def body(tokens, cotangent, w_qkv, w_out, w_up, w_down, gains, shifts, b_qkv, b_up, clip_lengths):
    own = w_up.shape[0]
    dp = D // own
    inner = dp == 8
    d = lax.axis_index("dp")
    wa = pack_heads(w_qkv[0], w_qkv[1], w_qkv[2], w_out.T)
    wu = w_up
    wd = w_down.T

    wide = jnp.concatenate([gains, shifts], axis=0)
    wide = lax.dynamic_update_slice(jnp.zeros((6, D), BF16), wide, (0, d * own))
    heads = b_qkv.shape[1]
    per_head = b_qkv.shape[2]
    full_head = per_head * dp
    bq = lax.dynamic_update_slice(
        jnp.zeros((2, heads, full_head), BF16), b_qkv, (0, 0, d * per_head)
    ).reshape(2, heads * full_head)
    none = jnp.zeros((heads * full_head,), BF16)
    bq = pack_heads(bq[0], none, bq[1], none)
    bu = lax.dynamic_update_slice(
        jnp.zeros((b_up.shape[0], b_up.shape[1] * dp), BF16), b_up, (0, d * b_up.shape[1])
    ).reshape(1, D)
    ws = jnp.concatenate([wide, bq[None], bu, jnp.zeros((8, D), BF16)], axis=0)

    if not inner:
        wa, wu, wd = (
            lax.all_gather(w, "dp", axis=0, tiled=True).reshape(PARTS, PIECE, D)
            for w in (wa, wu, wd)
        )
        ws = lax.psum(ws.astype(F32), "dp").astype(BF16)
    mixed, tgrad, ga, gu, gd, small = call_kernel(
        inner, tokens, cotangent, ws, wa, wu, wd, clip_lengths
    )
    if not inner:
        ga, gu, gd = (
            lax.psum_scatter(
                w.astype(F32).reshape(D, D), "dp", scatter_dimension=0, tiled=True
            )
            for w in (ga, gu, gd)
        )
        small = lax.psum(small, "dp")

    q, k, v, o = unpack_heads(ga)
    wide = lax.dynamic_slice(small[0:6], (0, d * own), (6, own))
    bq, _, bv, _ = unpack_heads(small[6])
    b_qkv_grad = jnp.stack([bq, bv]).reshape(2, heads, full_head)
    b_qkv_grad = lax.dynamic_slice(b_qkv_grad, (0, 0, d * per_head), (2, heads, per_head))
    b_up_grad = lax.dynamic_slice(
        small[7].reshape(b_up.shape[0], -1), (0, d * b_up.shape[1]), b_up.shape
    )
    return (
        mixed,
        tgrad,
        jnp.stack([q, k, v]),
        o.T,
        gu,
        gd.T,
        wide[0:2],
        wide[2:6],
        b_qkv_grad,
        b_up_grad,
    )


def solution(mesh):
    return jax.shard_map(
        body,
        mesh=mesh,
        in_specs=(
            P("dp", None),
            P("dp", None),
            P(None, "dp", "tp"),
            P("tp", "dp"),
            P("dp", "tp"),
            P("tp", "dp"),
            P(None, "dp"),
            P(None, "dp"),
            P(None, "tp", "dp"),
            P("tp", "dp"),
            P("dp", None),
        ),
        out_specs=(
            P("dp", None),
            P("dp", None),
            P(None, "dp", "tp"),
            P("tp", "dp"),
            P("dp", "tp"),
            P("tp", "dp"),
            P(None, "dp"),
            P(None, "dp"),
            P(None, "tp", "dp"),
            P("tp", "dp"),
        ),
        check_vma=False,
    )
```

time: 858 us -> 148 us (0.17)
  waiting for transfers between devices: 497 us -> 0 us
  blocking collectives: 183 us -> 0 us
  Pallas kernels: 0 us -> 126 us
  matrix products: 64.7 us -> 0 us
  other arithmetic: 40.9 us -> 2.23 us
  local copies, waits for them, and re-layouts: 45 us -> 18.4 us
  between operations: 18 us -> 0.84 us
    unnamed x18 -> x0, waiting for transfers between devices: 186 us -> none
    all_gather x6 -> x0, blocking collectives: 162 us -> none  [the longest x1 35.6 us: fetch_weights(): lax.all_gather(w_qkv, 'dp', axis=1, tiled=True)]
    reduce_scatter x2 -> x0, waiting for transfers between devices: 142 us -> none  [the longest x1 72 us: reduce_grads(): lax.psum_scatter(gradient[3], 'dp', scatter_dimension=1, tiled=True)]
    psum x4 -> x0, waiting for transfers between devices: 129 us -> none  [the longest x1 54.1 us: micro_step(): lax.psum(down_terms.astype(jnp.bfloat16), 'tp').astype(jnp.float32)]
    pallas_call x0 -> x1, Pallas kernels: none -> 126 us  [call_kernel(): pl.pallas_call(kernel, out_shape=(jax.ShapeDtypeStruct((rows, D), BF16),...]
    dot_general x34 -> x0, matrix products: 61.8 us -> none  [the longest x2 11.9 us: micro_step(): jnp.dot(normed_two_low, w_up, preferred_element_type=jnp.float32)]
    all_gather x2 -> x0, waiting for transfers between devices: 39.9 us -> none  [the longest x1 35.3 us: fetch_weights(): lax.all_gather(w_down, 'dp', axis=1, tiled=True)]
    unnamed x284 -> x17, local copies, waits for them, and re-layouts: 34.7 us -> 8.46 us
  transfers between devices with their start and end apart: 13 -> 0, of which waited for: 11 -> 0; matrix products, arithmetic and copies ran while one was open for 10% -> 0% of each run, Pallas kernels for 0% -> 0%
where the time goes in v1:
time: 148 us; the launch traced here: 147 us
  Pallas kernels  126 us (85%)
  local copies, waits for them, and re-layouts  18.4 us (12%)
  other arithmetic  2.23 us (2%)
    pallas_call x1, Pallas kernels, call_kernel(): pl.pallas_call(kernel, out_shape=(jax.ShapeDtypeStruct((rows, D), BF16),...  126 us
    unnamed x17, local copies, waits for them, and re-layouts  8.46 us

profile of v1, /device:TPU:0, one launch (start us, length us, event | category | flops | bytes accessed | tf_op | source)
XLA Modules:
  0.0 147.3 jit_solution(1968771014882286044)
XLA Ops:
  0.7 0.8 dynamic_update_slice.11
  1.5 0.7 copy.24
  2.2 0.1 dynamic_update_slice.10
  2.3 0.1 slice.131
  2.4 0.1 slice.133
  2.5 0.1 concatenate.32
  2.6 0.7 pad_maximum_fusion.1
  3.3 0.2 dynamic_update_slice.9
  3.5 0.1 pad.20.clone
  3.5 0.7 maximum_maximum_fusion.refs_2_
  4.2 0.9 slice_bitcast_fusion
  5.1 0.9 copy.25
  6.1 0.8 concatenate.34.refs_3_
  6.8 125.8 %shard_map.186 = (bf16[1024,768]{1,0:T(8,128)(2,1)}, f32[1024,768]{1,0:T(8,128)}, f32[96,768]{1,0:T(8,128)}, f32[96,768]{1,0:T(8,128)}, f32[96,768]{1,0:T(8,128)}, /*index=5*/f32[8,768]{1,0:T(8,128)}) custom-call(bf16[1024,768]{1,0:T(8,128)(2,1)} %refs_0_.1, bf16[1024,768]{1,0:T(8,128)(2,1)} %refs_1_.1, bf16[16,768]{1,0:T(8,128)(2,1)} %maximum_maximum_fusion.refs_2_, ...), custom_call_target="tpu_custom_call" | custom-call | tf_op jit(solution)/shard_map/pallas_call | solution.py:568
  132.6 0.0 copy-start.1
  132.6 1.1 fusion.1
  133.7 0.9 fusion
  134.7 0.7 pad_maximum_fusion
  135.4 0.7 copy.26
  136.2 0.8 constant_dynamic-slice_fusion.1
  136.9 0.6 slice.158
  137.5 0.6 slice.159
  138.1 0.7 slice_bitcast_fusion.7
  138.8 0.7 slice_bitcast_fusion.8
  139.4 0.1 stack.26
  139.5 0.1 stack.25
  139.6 0.1 dynamic-slice_maximum_fusion
  139.7 0.6 copy.27
  140.3 0.8 slice_reduce_fusion
  141.0 0.7 constant_dynamic-slice_fusion
  141.7 0.0 copy-done.1
  141.7 0.0 copy-start
  141.7 1.1 copy.38
  142.9 1.3 copy-done
  144.2 0.0 copy-start.3
  144.2 0.0 copy-start.2
  144.2 1.7 %copy.39 = f32[1024,768]{1,0:T(8,128)} copy(f32[1024,768]{1,0:T(8,128)S(1)} %copy-done) | data formatting | bytes 6291456
  145.8 0.0 copy-done.3
  145.8 0.7 copy.40
  146.6 0.0 copy-done.2
  146.6 0.7 copy.41
  (22 shorter events, 0.1 us)
Async XLA Ops:
  132.6 9.1 %copy-start.1 = (bf16[1024,768]{1,0:T(8,128)(2,1)S(1)}, bf16[1024,768]{1,0:T(8,128)(2,1)}, u32[]{:S(2)}) copy-start(bf16[1024,768]{1,0:T(8,128)(2,1)} %get-tuple-element.75) | copy-start | bytes 4718596
  141.7 2.5 %copy-start = (f32[1024,768]{1,0:T(8,128)S(1)}, f32[1024,768]{1,0:T(8,128)}, u32[]{:S(2)}) copy-start(f32[1024,768]{1,0:T(8,128)} %get-tuple-element.76) | copy-start | bytes 9437188
  144.2 1.7 %copy-start.3 = (f32[96,768]{1,0:T(8,128)S(1)}, f32[96,768]{1,0:T(8,128)}, u32[]{:S(2)}) copy-start(f32[96,768]{1,0:T(8,128)} %get-tuple-element.79) | copy-start | bytes 884740
  144.2 2.4 %copy-start.2 = (f32[96,768]{1,0:T(8,128)S(1)}, f32[96,768]{1,0:T(8,128)}, u32[]{:S(2)}) copy-start(f32[96,768]{1,0:T(8,128)} %get-tuple-element.20) | copy-start | bytes 884740

commit v2 on v1

--- a/solution.py
+++ b/solution.py
@@ -38,13 +38,19 @@
 
 
 def layer_kernel(inner, nb, refs):
-    (tok_h, cot_h, ws, wa, wu, wd, lens) = refs[:7]
-    (mixed_h, tgrad_h, gra_o, gru_o, grd_o, small_o) = refs[7:13]
+    if inner:
+        (tok_h, cot_h, w_qkv, w_out, wu, wd, gains, shifts, b_qkv, b_up, lens) = refs[:11]
+        wa, ws, wt = refs[-3:]
+        refs = refs[11:-3]
+    else:
+        (tok_h, cot_h, ws, wa, wu, wd, lens) = refs[:7]
+        refs = refs[7:]
+    (mixed_h, tgrad_h, gra_o, gru_o, grd_o, small_o) = refs[:6]
     (
         tok, cot, g, gs, prm, nrm, qh, kh, vh, pr, att, mid, n2, act, dgl, hg, ml, mgr, dqkv,
         dka, dva, pb, rc, sy, ry, mxs, tgs, gr, rx, hs, rz, sg, sgc, sgx, sgz,
         lsem, zss, zrs, xss, xrs, css, crs, yss, yrs, nss, nrs, oss, ors, rxs, rxr, rzs, rzr, sms, smr,
-    ) = refs[13:]
+    ) = refs[6:]
     d = lax.axis_index("dp")
     t = lax.axis_index("tp")
     z = d // 2
@@ -68,16 +74,61 @@
         later.append((copy.wait_send, guard))
 
     bar = pltpu.get_barrier_semaphore()
-    greet = [(d, sib), (d, yn)]
-    if inner:
-        greet += [(xn, t)] + [(lax.rem(d + 2 * j, 8), t) for j in (1, 2, 3)]
+    greet = [(d, sib), (d, yn)] + ([(xn, t)] if inner else [])
+    greeted = len(greet)
     for who in greet:
         pl.semaphore_signal(bar, 1, device_id=who, device_id_type=MESH)
+    if inner:
+        for guard, who in ((z < 3, d + 2), (z > 0, d - 2)):
+
+            @pl.when(guard)
+            def _():
+                pl.semaphore_signal(bar, 1, device_id=(who, t), device_id_type=MESH)
+
+            greeted = greeted + guard.astype(jnp.int32)
     cp_tok = pltpu.make_async_copy(tok_h, tok, lsem.at[0])
     cp_tok.start()
     cp_cot = pltpu.make_async_copy(cot_h, cot, lsem.at[1])
     cp_cot.start()
-    pl.semaphore_wait(bar, len(greet))
+    if inner:
+        def spot(rows, shift):
+            i = lax.broadcasted_iota(jnp.int32, (rows, 128), 0)
+            return (lax.broadcasted_iota(jnp.int32, (rows, 128), 1) == i + shift).astype(F32).astype(BF16)
+
+        for k in range(3):
+            wa[:, 128 * k : 128 * k + 128] = w_qkv[k, :, 0:128]
+        q2, k2, v2 = (w_qkv[k, :, 128:192] for k in range(3))
+        wa[:, 384:512] = (mm(q2, spot(64, 0), 1, 0) + mm(k2, spot(64, 64), 1, 0)).astype(BF16)
+        wa[:, 512:640] = (
+            mm(v2, spot(64, 0), 1, 0) + mm(w_out[128:192, :], spot(64, 64), 0, 0)
+        ).astype(BF16)
+        wa[:, 640:768] = mm(w_out[0:128, :], spot(128, 0), 0, 0).astype(BF16)
+        own = gains.shape[1]
+        wt[...] = jnp.zeros_like(wt)
+        wt[0:2, 0:own] = gains[...].astype(F32)
+        wt[2:6, 0:own] = shifts[...].astype(F32)
+        wide = pltpu.roll(wt[0:8], d * own, 1)
+        wt[...] = jnp.zeros_like(wt)
+        wt[0:8] = wide
+        per = b_up.shape[1]
+        sg[...] = jnp.zeros_like(sg)
+        sg[0:6, 0:per] = b_up[...].astype(F32)
+        turned = pltpu.roll(sg[0:8, 0:128], d * per, 1)
+        for k in range(6):
+            wt[7:8, 128 * k : 128 * k + 128] = turned[k : k + 1]
+        per = b_qkv.shape[2]
+        sg[...] = jnp.zeros_like(sg)
+        for h in range(3):
+            sg[h : h + 1, 0:per] = b_qkv[h, 0:1].astype(F32)
+            sg[3 + h : 4 + h, 0:per] = b_qkv[h, 1:2].astype(F32)
+        turned = pltpu.roll(sg[0:8, 0:128], d * per, 1)
+        other = pltpu.roll(turned, 64, 1)
+        wt[6:7, 0:128] = turned[0:1] + other[1:2]
+        wt[6:7, 256:384] = turned[3:4] + other[4:5]
+        wt[6:7, 384:512] = turned[2:3]
+        wt[6:7, 512:640] = turned[5:6]
+        ws[...] = wt[...].astype(BF16)
+    pl.semaphore_wait(bar, greeted)
 
     shards = (wa, wu, wd, ws)
 
@@ -90,9 +141,11 @@
     def xcopy(m, src, i, zsrc):
         return remote(src, slot(m, i), xss.at[m, zsrc], xrs.at[m, zsrc], xn, t)
 
-    def gather_start(m):
+    def gather_z(m):
         launch(zcopy(m, 0, shards[m], d, 0), z < 3)
         launch(zcopy(m, 1, shards[m], d, 0), z > 0)
+
+    def gather_x(m):
         launch(xcopy(m, shards[m], d, z))
 
     def gather_step(m, s):
@@ -296,7 +349,14 @@
         sg[6:7, 0:640] += jnp.sum(dqkv[blk, 0:640].astype(F32), axis=0, keepdims=True)
 
     def in_part(b):
-        sum_part(3, b, lambda rows: mm(dqkv[rows, 0:640], g[0, :, :, 0:640].reshape(D, 640), 1, 1))
+        def product(rows):
+            part = mm(dqkv[rows, 0:640], g[0, :, :, 0:640].reshape(D, 640), 1, 1)
+            zz, _ = standardize(tok[rows].astype(F32))
+            sg[0:1] += jnp.sum(part * zz, axis=0, keepdims=True)
+            sg[2:3] += jnp.sum(part, axis=0, keepdims=True)
+            return part
+
+        sum_part(3, b, product)
 
     def out_copies(k, buf, out, b):
         mine = pltpu.make_async_copy(buf.at[b], out.at[own_rows(b)], lsem.at[2 + 2 * k + b])
@@ -317,8 +377,6 @@
         zz, rstd = standardize(tok[own_rows(b)].astype(F32))
         tgs[b] = mgr[b] + norm_back(total, prm[0:1], zz, rstd)
         out_copies(1, tgs, tgrad_h, b)
-        sg[0:1] += jnp.sum(total * zz, axis=0, keepdims=True)
-        sg[2:3] += jnp.sum(total, axis=0, keepdims=True)
 
     def xred(m, k):
         return remote(gr.at[m, 2 * k + 1 - x], rx.at[m, k], rxs.at[m, k], rxr.at[m, k], xn, t)
@@ -373,120 +431,160 @@
             [a1[:, 0:512], a1[:, 512:640] + a2[:, 0:128], a2[:, 128:256]], axis=1
         )
 
+    row = lax.broadcasted_iota(jnp.int32, (8, 1), 0)
+
+    def small_c():
+        return remote(sg, sgc.at[0], sms.at[0], smr.at[0], d, sib)
+
+    def small_y():
+        return remote(sgc.at[1], sgc.at[2], sms.at[1], smr.at[1], d, yn)
+
+    def small_x():
+        return remote(sgx.at[0], sgx.at[1], sms.at[2], smr.at[2], xn, t)
+
+    def small_z(k):
+        return remote(
+            sgz.at[0], sgz.at[k], sms.at[2 + k], smr.at[2 + k], lax.rem(d + 2 * k, 8), t
+        )
+
+    def small_step(n):
+        if n == 0:
+            launch(small_c())
+        elif n == 1:
+            small_c().wait_recv()
+            sgc[1] = sg[...] + jnp.where(row < 6, sgc[0], 0.0)
+            launch(small_y())
+        elif n == 2:
+            small_y().wait_recv()
+            both = sgc[1] + jnp.where(jnp.logical_or(row == 0, row == 2), sgc[2], 0.0)
+            if inner:
+                sgx[0] = both
+                launch(small_x())
+            else:
+                small_o[...] = both
+        elif n == 3 and inner:
+            small_x().wait_recv()
+            sgz[0] = sgx[0] + sgx[1]
+            for k in (1, 2, 3):
+                launch(small_z(k))
+        elif n == 4 and inner:
+            for k in (1, 2, 3):
+                small_z(k).wait_recv()
+            small_o[...] = (sgz[0] + sgz[1]) + (sgz[2] + sgz[3])
+
     sg[...] = jnp.zeros_like(sg)
-    if inner:
-        gather_start(3)
-        gather_start(0)
-        for m in range(3):
-            cp = pltpu.make_async_copy(shards[m], g.at[m, d], lsem.at[6 + m])
-            cp.start()
-        cp = pltpu.make_async_copy(ws, gs.at[d], lsem.at[9])
-        cp.start()
-        for s in (1, 2, 3):
-            gather_step(3, s)
-        gather_start(1)
-        gather_end(3)
-        for m in range(3):
-            pltpu.make_async_copy(shards[m], g.at[m, d], lsem.at[6 + m]).wait()
-        cp.wait()
-        total = gs[0].astype(F32)
-        for i in range(1, PARTS):
-            total = total + gs[i].astype(F32)
-        prm[...] = total
-    else:
-        for m in range(3):
-            pltpu.make_async_copy(shards[m], g.at[m], lsem.at[6 + m]).start()
-        for m in range(3):
-            pltpu.make_async_copy(shards[m], g.at[m], lsem.at[6 + m]).wait()
-        prm[...] = ws[...].astype(F32)
+    own_pieces = []
+    for m in range(3 if not inner else 4):
+        own_pieces.append(
+            pltpu.make_async_copy(shards[m], slot(m, d) if inner else g.at[m], lsem.at[6 + m])
+        )
+
+    def add_parameters():
+        if inner:
+            own_pieces[3].wait()
+            gather_end(3)
+            total = gs[0].astype(F32)
+            for i in range(1, PARTS):
+                total = total + gs[i].astype(F32)
+            prm[...] = total
+        else:
+            prm[...] = ws[...].astype(F32)
 
     def step(m, s):
         if inner:
             gather_step(m, s)
 
+    if inner:
+        for m in (0, 3):
+            gather_z(m)
+            gather_x(m)
+    for cp in own_pieces:
+        cp.start()
     step(0, 1)
+    step(3, 1)
+    step(0, 2)
+    step(3, 2)
+    if inner:
+        gather_z(1)
+    step(0, 3)
+    step(3, 3)
+    if inner:
+        gather_x(1)
+    add_parameters()
     cp_tok.wait()
-    cp_cot.wait()
-    for b in range(nb):
+    first_norm(0)
+    step(1, 1)
+    if inner:
+        gather_z(2)
+    for b in range(1, nb):
         first_norm(b)
-    step(0, 2)
-    step(0, 3)
-    if inner:
-        gather_start(2)
+    for cp in own_pieces[:3]:
+        cp.wait()
+    if inner:
         gather_end(0)
-    pumps = [(1, 1), (1, 2), (1, 3), (2, 1), (2, 2), (2, 3)]
-
-    def pump():
-        if pumps:
-            step(*pumps.pop(0))
-
+    step(1, 2)
     for b in range(nb):
         project(b)
+        if b:
+            sum_mid(0, b - 1)
+            step(2, 1)
+        else:
+            step(1, 3)
+            if inner:
+                gather_x(2)
         attend(b)
-        pump()
         out_part(b)
-        pump()
-        sum_mid(0, b)
-        pump()
-    while pumps:
-        pump()
+    cp_cot.wait()
+    sum_mid(0, nb - 1)
+    step(2, 2)
+    step(2, 3)
     if inner:
         gather_end(1)
     for b in range(nb):
         second_norm(b)
         shared(n2, 0, b)
         up(b)
-    if inner:
-        gather_end(2)
-    for b in range(nb):
+        if inner and b == 0:
+            gather_end(2)
         hidden_back(b)
         sum_part(2, b, lambda rows: mm(hg[rows], mat(1), 1, 1))
-        if b > 0:
-            sum_mid(2, b - 1)
-    sum_mid(2, nb - 1)
-    for b in range(nb):
+        if b == 0:
+            sum_part(1, b, lambda rows: mm(act[rows], mat(2), 1, 1))
+        sum_mid(2, b)
+    sum_mid(1, 0)
+    weight_grad(2, down_grad)
+    for b in range(1, nb):
         sum_part(1, b, lambda rows: mm(act[rows], mat(2), 1, 1))
-    weight_grad(2, down_grad)
-    for b in range(nb):
-        sum_mid(1, b)
     weight_grad(1, up_grad)
     for b in range(nb):
         middle_back(b)
         shared(ml, 1, b)
         attend_back(b)
+        if b == nb - 1:
+            weight_grad(0, in_grad)
         in_part(b)
+        if b == nb - 1:
+            small_step(0)
+            small_step(1)
+        sum_mid(3, b)
         if b == 0:
             reduce_mid(2)
-        sum_mid(3, b)
-    weight_grad(0, in_grad)
+    for b in range(1, nb):
+        sum_mid(1, b)
     reduce_mid(1)
-    for b in range(nb):
-        finish_mixed(b)
+    finish_mixed(0)
+    finish_tokens(0)
+    small_step(2)
     reduce_mid(0)
-    for b in range(nb):
+    for b in range(1, nb):
         finish_tokens(b)
-    smc = remote(sg, sgc, sms.at[0], smr.at[0], d, sib)
-    smc.start()
+    small_step(3)
     reduce_end(2)
     reduce_end(1)
-    smc.wait()
-    row = lax.broadcasted_iota(jnp.int32, (8, 1), 0)
-    total = sg[...] + jnp.where(row < 6, sgc[...], 0.0)
-    if inner:
-        sgx[0] = total
-        smx = remote(sgx.at[0], sgx.at[1], sms.at[1], smr.at[1], xn, t)
-        smx.start()
-        smx.wait()
-        sgz[0] = sgx[0] + sgx[1]
-        for k in (1, 2, 3):
-            launch(remote(sgz.at[0], sgz.at[k], sms.at[1 + k], smr.at[1 + k], lax.rem(d + 2 * k, 8), t))
-        reduce_end(0)
-        for k in (1, 2, 3):
-            remote(sgz.at[0], sgz.at[k], sms.at[1 + k], smr.at[1 + k], xn, t).wait_recv()
-        small_o[...] = (sgz[0] + sgz[1]) + (sgz[2] + sgz[3])
-    else:
-        small_o[...] = total
-        reduce_end(0)
+    small_step(4)
+    reduce_end(0)
+    for b in range(1, nb):
+        finish_mixed(b)
     for wait, guard in later:
         if guard is None:
             wait()
@@ -494,8 +592,8 @@
             pl.when(guard)(wait)
 
 
-def call_kernel(inner, tokens, cotangent, ws, wa, wu, wd, lens):
-    rows = tokens.shape[0]
+def call_kernel(inner, *args):
+    rows = args[0].shape[0]
     nb = rows // BLK
     vmem = pl.BlockSpec(memory_space=pltpu.VMEM)
     anywhere = pl.BlockSpec(memory_space=pl.ANY)
@@ -538,7 +636,7 @@
         pltpu.VMEM((3, 4, PIECE, D), BF16),
         pltpu.VMEM((3, 3, PIECE, D), BF16),
         pltpu.VMEM((8, D), F32),
-        pltpu.VMEM((8, D), F32),
+        pltpu.VMEM((3, 8, D), F32),
         pltpu.VMEM((2, 8, D), F32),
         pltpu.VMEM((4, 8, D), F32),
         dma((10,)),
@@ -558,9 +656,11 @@
         dma((3, 4)),
         dma((3, 3)),
         dma((3, 3)),
-        dma((5,)),
-        dma((5,)),
+        dma((6,)),
+        dma((6,)),
     ]
+    if inner:
+        scratch += [pltpu.VMEM((PIECE, D), BF16), pltpu.VMEM((16, D), BF16), pltpu.VMEM((16, D), F32)]
 
     def kernel(*refs):
         layer_kernel(inner, nb, refs)
@@ -575,13 +675,15 @@
             grads,
             jax.ShapeDtypeStruct((8, D), F32),
         ),
-        in_specs=[anywhere, anywhere, vmem, vmem, vmem, vmem, pl.BlockSpec(memory_space=pltpu.SMEM)],
+        in_specs=[anywhere, anywhere]
+        + ([vmem, vmem, anywhere, anywhere, vmem, vmem, vmem, vmem] if inner else [vmem] * 4)
+        + [pl.BlockSpec(memory_space=pltpu.SMEM)],
         out_specs=(anywhere, anywhere, vmem, vmem, vmem, vmem),
         scratch_shapes=scratch,
         compiler_params=pltpu.CompilerParams(
             collective_id=0, has_side_effects=True, vmem_limit_bytes=60 * 2**20
         ),
-    )(tokens, cotangent, ws, wa, wu, wd, lens)
+    )(*args)
 
 
 def pack_heads(q, k, v, o):
@@ -602,15 +704,74 @@
     return q, k, v, o
 
 
+def unpack_kernel(mix_h, tok_h, ga, gu, gd, small, mix_o, tok_o, qkv_o, out_o, up_o, down_o, gains_o, shifts_o, bqkv_o, bup_o, tok_v, mix_v, sem):
+    d = lax.axis_index("dp")
+    moves = []
+    for src, via, dst in ((tok_h, tok_v, tok_o), (mix_h, mix_v, mix_o)):
+        for k in range(4):
+            rows = slice(k * src.shape[0] // 4, (k + 1) * src.shape[0] // 4)
+            sems = sem.at[len(moves)]
+            load = pltpu.make_async_copy(src.at[rows], via.at[rows], sems)
+            load.start()
+            moves.append((load, pltpu.make_async_copy(via.at[rows], dst.at[rows], sems)))
+    for load, store in moves:
+        load.wait()
+        store.start()
+    own = gains_o.shape[1]
+    for k in range(3):
+        qkv_o[k, :, 0:128] = ga[:, 128 * k : 128 * k + 128]
+    qkv_o[0, :, 128:192] = ga[:, 384:448]
+    qkv_o[1, :, 128:192] = pltpu.roll(ga[:, 384:512], 64, 1)[:, 0:64]
+    qkv_o[2, :, 128:192] = ga[:, 512:576]
+    fill = jnp.zeros((128 - own, 128), F32)
+    out_o[0:128, :] = jnp.concatenate([ga[:, 640:768], fill], axis=0).T[:, 0:own]
+    out_o[128:192, :] = jnp.concatenate([ga[:, 512:640], fill], axis=0).T[64:128, 0:own]
+    up_o[...] = gu[...]
+    down_o[...] = gd[...]
+    wide = pltpu.roll(small[...], D - d * own, 1)
+    gains_o[...] = wide[0:2, 0:own]
+    shifts_o[...] = wide[2:6, 0:own]
+    for part in range(2):
+        for h, at in enumerate((0, 64, 384) if part == 0 else (256, 320, 512)):
+            per = bqkv_o.shape[2]
+            slab = small[:, at // 128 * 128 : at // 128 * 128 + 128]
+            turned = pltpu.roll(slab, 128 - at % 128 - d * per + 128 * (at % 128 // 64), 1)
+            bqkv_o[h, part : part + 1, :] = turned[6:7, 0:per]
+    for k in range(6):
+        per = bup_o.shape[1]
+        turned = pltpu.roll(small[:, 128 * k : 128 * k + 128], 128 - d * per, 1)
+        bup_o[k : k + 1, :] = turned[7:8, 0:per]
+    for _, store in moves:
+        store.wait()
+
+
 def body(tokens, cotangent, w_qkv, w_out, w_up, w_down, gains, shifts, b_qkv, b_up, clip_lengths):
     own = w_up.shape[0]
     dp = D // own
-    inner = dp == 8
+    if dp == 8:
+        mixed, tgrad, ga, gu, gd, small = call_kernel(
+            True, tokens, cotangent, w_qkv, w_out, w_up, w_down.T,
+            gains, shifts, b_qkv.transpose(1, 0, 2), b_up, clip_lengths,
+        )
+        vmem = pl.BlockSpec(memory_space=pltpu.VMEM)
+        anywhere = pl.BlockSpec(memory_space=pl.ANY)
+        like = [mixed, tgrad, w_qkv, w_out, gu, gd, gains, shifts, b_qkv.transpose(1, 0, 2), b_up]
+        outs = pl.pallas_call(
+            unpack_kernel,
+            out_shape=tuple(
+                jax.ShapeDtypeStruct(a.shape, BF16 if i == 0 else F32) for i, a in enumerate(like)
+            ),
+            in_specs=[anywhere, anywhere] + [vmem] * 4,
+            out_specs=tuple([anywhere, anywhere] + [vmem] * 8),
+            scratch_shapes=[
+                pltpu.VMEM(tgrad.shape, F32),
+                pltpu.VMEM(mixed.shape, BF16),
+                pltpu.SemaphoreType.DMA((8,)),
+            ],
+        )(mixed, tgrad, ga, gu, gd, small)
+        return outs[:5] + (outs[5].T, outs[6], outs[7], outs[8].transpose(1, 0, 2), outs[9])
+
     d = lax.axis_index("dp")
-    wa = pack_heads(w_qkv[0], w_qkv[1], w_qkv[2], w_out.T)
-    wu = w_up
-    wd = w_down.T
-
     wide = jnp.concatenate([gains, shifts], axis=0)
     wide = lax.dynamic_update_slice(jnp.zeros((6, D), BF16), wide, (0, d * own))
     heads = b_qkv.shape[1]
@@ -625,25 +786,20 @@
         jnp.zeros((b_up.shape[0], b_up.shape[1] * dp), BF16), b_up, (0, d * b_up.shape[1])
     ).reshape(1, D)
     ws = jnp.concatenate([wide, bq[None], bu, jnp.zeros((8, D), BF16)], axis=0)
-
-    if not inner:
-        wa, wu, wd = (
-            lax.all_gather(w, "dp", axis=0, tiled=True).reshape(PARTS, PIECE, D)
-            for w in (wa, wu, wd)
-        )
-        ws = lax.psum(ws.astype(F32), "dp").astype(BF16)
+    ws = lax.psum(ws.astype(F32), "dp").astype(BF16)
+    wa = pack_heads(w_qkv[0], w_qkv[1], w_qkv[2], w_out.T)
+    wa, wu, wd = (
+        lax.all_gather(w, "dp", axis=0, tiled=True).reshape(PARTS, PIECE, D)
+        for w in (wa, w_up, w_down.T)
+    )
     mixed, tgrad, ga, gu, gd, small = call_kernel(
-        inner, tokens, cotangent, ws, wa, wu, wd, clip_lengths
+        False, tokens, cotangent, ws, wa, wu, wd, clip_lengths
     )
-    if not inner:
-        ga, gu, gd = (
-            lax.psum_scatter(
-                w.astype(F32).reshape(D, D), "dp", scatter_dimension=0, tiled=True
-            )
-            for w in (ga, gu, gd)
-        )
-        small = lax.psum(small, "dp")
-
+    ga, gu, gd = (
+        lax.psum_scatter(w.astype(F32).reshape(D, D), "dp", scatter_dimension=0, tiled=True)
+        for w in (ga, gu, gd)
+    )
+    small = lax.psum(small, "dp")
     q, k, v, o = unpack_heads(ga)
     wide = lax.dynamic_slice(small[0:6], (0, d * own), (6, own))
     bq, _, bv, _ = unpack_heads(small[6])

time: 148 us -> 127 us (0.86)
  local copies, waits for them, and re-layouts: 18.4 us -> 0 us
  other arithmetic: 2.23 us -> 0 us
    unnamed x17 -> x0, local copies, waits for them, and re-layouts: 8.46 us -> none
    pallas_call x0 -> x1, Pallas kernels: none -> 5.87 us  [body(): pl.pallas_call(unpack_kernel, out_shape=tuple((jax.ShapeDtypeStruct(a.sha...]
    pallas_call x1, Pallas kernels: 126 us -> 120 us  [call_kernel(): pl.pallas_call(kernel, out_shape=(jax.ShapeDtypeStruct((rows, D), BF16),...]
    slice x19 -> x0, local copies, waits for them, and re-layouts: 5.44 us -> none  [the longest x2 1.97 us: unpack_heads(): o = jnp.concatenate([w[..., 640:768], w[..., 576:640]], axis=-1)]
where the time goes in v2:
time: 127 us
  Pallas kernels  126 us (99%)
    pallas_call x1, Pallas kernels, call_kernel(): pl.pallas_call(kernel, out_shape=(jax.ShapeDtypeStruct((rows, D), BF16),...  120 us
    pallas_call x1, Pallas kernels, body(): pl.pallas_call(unpack_kernel, out_shape=tuple((jax.ShapeDtypeStruct(a.sha...  5.87 us

profile of v2, /device:TPU:0, one launch (start us, length us, event | category | flops | bytes accessed | tf_op | source)
XLA Modules:
  0.0 126.7 jit_solution(8724960300143065696)
XLA Ops:
  0.6 120.0 %shard_map.186 = (bf16[1024,768]{1,0:T(8,128)(2,1)}, f32[1024,768]{1,0:T(8,128)}, f32[96,768]{1,0:T(8,128)}, f32[96,768]{1,0:T(8,128)}, f32[96,768]{1,0:T(8,128)}, /*index=5*/f32[8,768]{1,0:T(8,128)}) custom-call(bf16[1024,768]{1,0:T(8,128)(2,1)} %refs_0_.1, bf16[1024,768]{1,0:T(8,128)(2,1)} %refs_1_.1, bf16[3,96,192]{2,1,0:T(8,128)(2,1)} %refs_2_.1, ...), custom_call_target="tpu_custom_call" | custom-call | tf_op jit(solution)/shard_map/pallas_call | solution.py:668
  120.7 5.9 %shard_map.187 = (bf16[1024,768]{1,0:T(8,128)(2,1)}, f32[1024,768]{1,0:T(8,128)}, f32[3,96,192]{2,1,0:T(8,128)}, f32[192,96]{1,0:T(8,128)}, f32[96,768]{1,0:T(8,...) custom-call(bf16[1024,768]{1,0:T(8,128)(2,1)} %get-tuple-element.26.m, ...), custom_call_target="tpu_custom_call" | custom-call | tf_op jit(solution)/shard_map/pallas_call | solution.py:759

commit v3 on v2

--- a/solution.py
+++ b/solution.py
@@ -48,7 +48,7 @@
     (mixed_h, tgrad_h, gra_o, gru_o, grd_o, small_o) = refs[:6]
     (
         tok, cot, g, gs, prm, nrm, qh, kh, vh, pr, att, mid, n2, act, dgl, hg, ml, mgr, dqkv,
-        dka, dva, pb, rc, sy, ry, mxs, tgs, gr, rx, hs, rz, sg, sgc, sgx, sgz,
+        dka, dva, pb, rc, ry, mxs, gr, rx, hs, rz, sg, sgc, sgx, sgz,
         lsem, zss, zrs, xss, xrs, css, crs, yss, yrs, nss, nrs, oss, ors, rxs, rxr, rzs, rzr, sms, smr,
     ) = refs[6:]
     d = lax.axis_index("dp")
@@ -177,7 +177,7 @@
         return remote(pb.at[st, b, 0], rc.at[st, b], css.at[st, b], crs.at[st, b], d, sib)
 
     def ycopy(st, b):
-        return remote(sy.at[st, b], ry.at[st, b], yss.at[st, b], yrs.at[st, b], d, yn)
+        return remote(pb.at[st, b, 1], ry.at[st, b], yss.at[st, b], yrs.at[st, b], d, yn)
 
     def sum_part(st, b, product):
         def one(j, carry):
@@ -194,12 +194,12 @@
 
     def sum_mid(st, b):
         ccopy(st, b).wait_recv()
-        sy[st, b] = (pb[st, b, 1].astype(F32) + rc[st, b].astype(F32)).astype(BF16)
+        pb[st, b, 1] = (pb[st, b, 1].astype(F32) + rc[st, b].astype(F32)).astype(BF16)
         launch(ycopy(st, b))
 
     def sum_end(st, b):
         ycopy(st, b).wait_recv()
-        return sy[st, b].astype(F32) + ry[st, b].astype(F32)
+        return pb[st, b, 1].astype(F32) + ry[st, b].astype(F32)
 
     def share(buf, k, b):
         return remote(buf.at[own_rows(b)], buf.at[own_rows(b)], nss.at[k, b], nrs.at[k, b], d, sib)
@@ -214,8 +214,12 @@
     def mat(m):
         return g[m].reshape(D, D)
 
-    def chunks(b, n, fn):
-        def one(i, carry):
+    def chunks(b, n, fn, ready=None):
+        def one(k, carry):
+            i = k
+            if ready is not None:
+                pl.when(k == n // 2)(ready)
+                i = lax.rem(c + k // (n // 2), 2) * (n // 2) + lax.rem(k, n // 2)
             fn(pl.ds(pl.multiple_of(b * BLK + i * (BLK // n), BLK // n), BLK // n), i)
             return carry
 
@@ -255,19 +259,19 @@
             )
 
         def fn(rows, i):
-            q_clip = clip_of(lax.broadcasted_iota(jnp.int32, (HALF, 1), 0) + i * HALF)
-            k_clip = clip_of(lax.broadcasted_iota(jnp.int32, (1, BLK), 1))
+            q_clip = clip_of(lax.broadcasted_iota(jnp.int32, (1, HALF), 1) + i * HALF)
+            k_clip = clip_of(lax.broadcasted_iota(jnp.int32, (BLK, 1), 0))
             same = q_clip == k_clip
             outs = []
             for h in range(3):
-                s = mm(qh[h, rows], kh[h, blk], 1, 1) * 0.125
+                s = mm(kh[h, blk], qh[h, rows], 1, 1) * 0.125
                 s = jnp.where(same, s, masked)
-                e = jnp.exp(s - jnp.max(s, axis=-1, keepdims=True))
-                p = (e / jnp.sum(e, axis=-1, keepdims=True)).astype(BF16)
-                pr[3 * b + h, pl.ds(pl.multiple_of(i * HALF, HALF), HALF)] = p
-                outs.append(mm(p, vh[h, blk], 1, 0))
-            att[rows, 0:128] = pltpu.roll(outs[2], 64, 1).astype(BF16)
-            att[rows, 128:256] = (outs[0] + outs[1]).astype(BF16)
+                e = jnp.exp(s - jnp.max(s, axis=0, keepdims=True))
+                p = (e / jnp.sum(e, axis=0, keepdims=True)).astype(BF16)
+                pr[3 * b + h, :, pl.ds(pl.multiple_of(i * HALF, HALF), HALF)] = p
+                outs.append(mm(vh[h, blk], p, 0, 0))
+            att[rows, 0:128] = pltpu.roll(outs[2], 64, 0).T.astype(BF16)
+            att[rows, 128:256] = (outs[0] + outs[1]).T.astype(BF16)
 
         chunks(b, 2, fn)
 
@@ -289,16 +293,16 @@
             act[rows] = (h * cdf).astype(BF16)
             dgl[rows] = cdf + h * (jnp.exp(-0.5 * h * h) * (1.0 / math.sqrt(2.0 * math.pi)))
 
-        chunks(b, 4, fn)
+        chunks(b, 4, fn, lambda: shared(n2, 0, b))
 
     def hidden_back(b):
-        def fn(rows, i):
-            hgr = mm(cot[rows], mat(2), 1, 0) * dgl[rows]
-            low_grad = hgr.astype(BF16)
+        def product(rows):
+            low_grad = (mm(cot[rows], mat(2), 1, 0) * dgl[rows]).astype(BF16)
             hg[rows] = low_grad
             sg[7:8] += jnp.sum(low_grad.astype(F32), axis=0, keepdims=True)
-
-        chunks(b, 2, fn)
+            return mm(low_grad, mat(1), 1, 1)
+
+        sum_part(2, b, product)
 
     def middle_back(b):
         rows = own_rows(b)
@@ -329,17 +333,17 @@
             )
             dqs = []
             for h in range(3):
-                p = pr[3 * b + h, pl.ds(pl.multiple_of(i * HALF, HALF), HALF)]
+                p = pr[3 * b + h, :, pl.ds(pl.multiple_of(i * HALF, HALF), HALF)]
                 pf = p.astype(F32)
-                dp = mm(dos[h], vh[h, blk], 1, 1)
-                ds = (pf * (dp - jnp.sum(pf * dp, axis=-1, keepdims=True))).astype(BF16)
-                dqs.append(mm(ds, kh[h, blk], 1, 0))
-                dka[h] += mm(ds, qh[h, rows], 0, 0)
-                dva[h] += mm(p, dos[h], 0, 0)
-            dqkv[rows, 0:128] = ((dqs[0] + dqs[1]) * 0.125).astype(BF16)
-            dqkv[rows, 384:512] = (dqs[2] * 0.125).astype(BF16)
-
-        chunks(b, 2, fn)
+                dp = mm(vh[h, blk], dos[h], 1, 1)
+                ds = (pf * (dp - jnp.sum(pf * dp, axis=0, keepdims=True))).astype(BF16)
+                dqs.append(mm(kh[h, blk], ds, 0, 0))
+                dka[h] += mm(ds, qh[h, rows], 1, 0)
+                dva[h] += mm(p, dos[h], 1, 0)
+            dqkv[rows, 0:128] = ((dqs[0] + dqs[1]) * 0.125).T.astype(BF16)
+            dqkv[rows, 384:512] = (dqs[2] * 0.125).T.astype(BF16)
+
+        chunks(b, 2, fn, lambda: shared(ml, 1, b))
         dqkv[blk, 128:256] = ((dka[0] + dka[1]) * 0.125).astype(BF16)
         dqkv[blk, 256:384] = (dva[0] + dva[1]).astype(BF16)
         dqkv[blk, 384:512] = (
@@ -375,48 +379,69 @@
     def finish_tokens(b):
         total = sum_end(3, b)
         zz, rstd = standardize(tok[own_rows(b)].astype(F32))
-        tgs[b] = mgr[b] + norm_back(total, prm[0:1], zz, rstd)
-        out_copies(1, tgs, tgrad_h, b)
-
-    def xred(m, k):
-        return remote(gr.at[m, 2 * k + 1 - x], rx.at[m, k], rxs.at[m, k], rxr.at[m, k], xn, t)
-
-    def zred(m, k, zd):
+        mgr[b] = mgr[b] + norm_back(total, prm[0:1], zz, rstd)
+        out_copies(1, mgr, tgrad_h, b)
+
+    def cut(q):
+        return slice(384 * q, 384 * q + 384)
+
+    def xred(m, q, k):
         return remote(
-            hs.at[m, zd], rz.at[m, k - 1], rzs.at[m, k - 1], rzr.at[m, k - 1], 2 * zd + x, t
+            gr.at[m, 2 * k + 1 - x, :, cut(q)], rx.at[m, k, :, cut(q)],
+            rxs.at[m, q, k], rxr.at[m, q, k], xn, t,
+        )
+
+    zp = z + 1 - 2 * lax.rem(z, 2)
+    zf = lax.rem(z + 2, 4)
+    zpf = lax.rem(zp + 2, 4)
+
+    def zred(m, q, k):
+        src, to = ((zp, zp), (zpf, zp), (zf, zf))[k]
+        return remote(
+            hs.at[m, src, :, cut(q)], rz.at[m, k, :, cut(q)],
+            rzs.at[m, q, k], rzr.at[m, q, k], 2 * to + x, t,
         )
 
     def weight_grad(m, product):
         for half in range(2):
-            gr[m, 4 * half : 4 * half + 4] = (
-                product(slice(384 * half, 384 * half + 384)).astype(BF16).reshape(4, PIECE, D)
-            )
-            if inner:
-                for k in (2 * half, 2 * half + 1):
-                    launch(xred(m, k))
+            gr[m, 4 * half : 4 * half + 4] = product(cut(half)).astype(BF16).reshape(4, PIECE, D)
+
+    def reduce_start(m, q):
+        if inner:
+            for k in range(4):
+                launch(xred(m, q, k))
 
     outs = (gra_o, gru_o, grd_o)
 
-    def reduce_mid(m):
+    def reduce_mid(m, q):
         if not inner:
             return
-        for k in (2, 1, 3, 0):
-            zd = lax.rem(z + k, 4)
-            xred(m, zd).wait_recv()
-            both = gr[m, 2 * zd + x].astype(F32) + rx[m, zd].astype(F32)
-            if k:
-                hs[m, zd] = both.astype(BF16)
-                launch(zred(m, k, zd))
+        for k, zd in ((1, zpf), (0, zp), (2, zf), (3, z)):
+            xred(m, q, zd).wait_recv()
+            both = gr[m, 2 * zd + x, :, cut(q)].astype(F32) + rx[m, zd, :, cut(q)].astype(F32)
+            if k < 3:
+                hs[m, zd, :, cut(q)] = both.astype(BF16)
             else:
-                outs[m][...] = both
+                outs[m][:, cut(q)] = both
+            if k < 2:
+                launch(zred(m, q, k))
+
+    def reduce_far(m, q):
+        if not inner:
+            return
+        zred(m, q, 1).wait_recv()
+        far = hs[m, zf, :, cut(q)].astype(F32) + rz[m, 1, :, cut(q)].astype(F32)
+        hs[m, zf, :, cut(q)] = far.astype(BF16)
+        launch(zred(m, q, 2))
 
     def reduce_end(m):
         if not inner:
             outs[m][...] = gr[m]
             return
-        for k in (1, 3, 2):
-            zred(m, k, lax.rem(z + k, 4)).wait_recv()
-            outs[m][...] += rz[m, k - 1].astype(F32)
+        for q in range(2):
+            zred(m, q, 0).wait_recv()
+            zred(m, q, 2).wait_recv()
+            outs[m][:, cut(q)] += rz[m, 0, :, cut(q)].astype(F32) + rz[m, 2, :, cut(q)].astype(F32)
 
     def down_grad(cols):
         return mm(cot[:, cols], act[...], 0, 0)
@@ -542,42 +567,56 @@
         gather_end(1)
     for b in range(nb):
         second_norm(b)
-        shared(n2, 0, b)
         up(b)
         if inner and b == 0:
             gather_end(2)
+        if b == nb - 1:
+            weight_grad(2, down_grad)
+            reduce_start(2, 0)
+            reduce_start(2, 1)
         hidden_back(b)
-        sum_part(2, b, lambda rows: mm(hg[rows], mat(1), 1, 1))
         if b == 0:
             sum_part(1, b, lambda rows: mm(act[rows], mat(2), 1, 1))
         sum_mid(2, b)
-    sum_mid(1, 0)
-    weight_grad(2, down_grad)
     for b in range(1, nb):
         sum_part(1, b, lambda rows: mm(act[rows], mat(2), 1, 1))
     weight_grad(1, up_grad)
     for b in range(nb):
         middle_back(b)
-        shared(ml, 1, b)
         attend_back(b)
+        if b == 0:
+            sum_mid(1, 0)
         if b == nb - 1:
             weight_grad(0, in_grad)
+            reduce_start(0, 1)
+            reduce_start(0, 0)
+            for q in range(2):
+                reduce_far(2, q)
         in_part(b)
         if b == nb - 1:
             small_step(0)
             small_step(1)
         sum_mid(3, b)
         if b == 0:
-            reduce_mid(2)
+            reduce_start(1, 0)
+            reduce_start(1, 1)
+            for q in range(2):
+                reduce_mid(2, q)
     for b in range(1, nb):
         sum_mid(1, b)
-    reduce_mid(1)
+    for q in range(2):
+        reduce_mid(1, q)
     finish_mixed(0)
     finish_tokens(0)
+    for q in range(2):
+        reduce_far(1, q)
     small_step(2)
-    reduce_mid(0)
+    reduce_mid(0, 1)
+    reduce_mid(0, 0)
     for b in range(1, nb):
         finish_tokens(b)
+    reduce_far(0, 1)
+    reduce_far(0, 0)
     small_step(3)
     reduce_end(2)
     reduce_end(1)
@@ -628,9 +667,7 @@
         pltpu.VMEM((4, nb, 2, HALF, D), BF16),
         pltpu.VMEM((4, nb, HALF, D), BF16),
         pltpu.VMEM((4, nb, HALF, D), BF16),
-        pltpu.VMEM((4, nb, HALF, D), BF16),
         pltpu.VMEM((nb, HALF, D), BF16),
-        pltpu.VMEM((nb, HALF, D), F32),
         pltpu.VMEM((3, PARTS, PIECE, D), BF16),
         pltpu.VMEM((3, 4, PIECE, D), BF16),
         pltpu.VMEM((3, 4, PIECE, D), BF16),
@@ -652,10 +689,10 @@
         dma((2, nb)),
         dma((2, nb)),
         dma((2, nb)),
-        dma((3, 4)),
-        dma((3, 4)),
-        dma((3, 3)),
-        dma((3, 3)),
+        dma((3, 2, 4)),
+        dma((3, 2, 4)),
+        dma((3, 2, 3)),
+        dma((3, 2, 3)),
         dma((6,)),
         dma((6,)),
     ]

time: 127 us -> 122 us (0.961)
  Pallas kernels: 126 us -> 120 us
    pallas_call x1, Pallas kernels: 120 us -> 114 us  [call_kernel(): pl.pallas_call(kernel, out_shape=(jax.ShapeDtypeStruct((rows, D), BF16),...]
where the time goes in v3:
time: 122 us; the launch traced here: 121 us
  Pallas kernels  120 us (98%)
    pallas_call x1, Pallas kernels, call_kernel(): pl.pallas_call(kernel, out_shape=(jax.ShapeDtypeStruct((rows, D), BF16),...  114 us
    pallas_call x1, Pallas kernels, body(): pl.pallas_call(unpack_kernel, out_shape=tuple((jax.ShapeDtypeStruct(a.sha...  5.87 us

profile of v3, /device:TPU:0, one launch (start us, length us, event | category | flops | bytes accessed | tf_op | source)
XLA Modules:
  0.0 120.7 jit_solution(14868829855923789636)
XLA Ops:
  0.6 114.0 %shard_map.186 = (bf16[1024,768]{1,0:T(8,128)(2,1)}, f32[1024,768]{1,0:T(8,128)}, f32[96,768]{1,0:T(8,128)}, f32[96,768]{1,0:T(8,128)}, f32[96,768]{1,0:T(8,128)}, /*index=5*/f32[8,768]{1,0:T(8,128)}) custom-call(bf16[1024,768]{1,0:T(8,128)(2,1)} %refs_0_.1, bf16[1024,768]{1,0:T(8,128)(2,1)} %refs_1_.1, bf16[3,96,192]{2,1,0:T(8,128)(2,1)} %refs_2_.1, ...), custom_call_target="tpu_custom_call" | custom-call | tf_op jit(solution)/shard_map/pallas_call | solution.py:705
  114.7 5.9 %shard_map.187 = (bf16[1024,768]{1,0:T(8,128)(2,1)}, f32[1024,768]{1,0:T(8,128)}, f32[3,96,192]{2,1,0:T(8,128)}, f32[192,96]{1,0:T(8,128)}, f32[96,768]{1,0:T(8,...) custom-call(bf16[1024,768]{1,0:T(8,128)(2,1)} %get-tuple-element.26.m, ...), custom_call_target="tpu_custom_call" | custom-call | tf_op jit(solution)/shard_map/pallas_call | solution.py:796

commit v4 on v3

--- a/solution.py
+++ b/solution.py
@@ -548,20 +548,20 @@
     if inner:
         gather_end(0)
     step(1, 2)
-    for b in range(nb):
-        project(b)
-        if b:
-            sum_mid(0, b - 1)
-            step(2, 1)
-        else:
-            step(1, 3)
-            if inner:
-                gather_x(2)
-        attend(b)
-        out_part(b)
+    project(0)
+    attend(0)
+    out_part(0)
+    step(1, 3)
+    if inner:
+        gather_x(2)
+    sum_mid(0, 0)
+    step(2, 1)
+    project(1)
+    attend(1)
+    out_part(1)
+    step(2, 2)
     cp_cot.wait()
-    sum_mid(0, nb - 1)
-    step(2, 2)
+    sum_mid(0, 1)
     step(2, 3)
     if inner:
         gather_end(1)
@@ -586,6 +586,8 @@
         attend_back(b)
         if b == 0:
             sum_mid(1, 0)
+            reduce_start(1, 0)
+            reduce_start(1, 1)
         if b == nb - 1:
             weight_grad(0, in_grad)
             reduce_start(0, 1)
@@ -598,8 +600,6 @@
             small_step(1)
         sum_mid(3, b)
         if b == 0:
-            reduce_start(1, 0)
-            reduce_start(1, 1)
             for q in range(2):
                 reduce_mid(2, q)
     for b in range(1, nb):

time: 122 us -> 118 us (0.967)
  Pallas kernels: 120 us -> 116 us
    pallas_call x1, Pallas kernels: 114 us -> 110 us  [call_kernel(): pl.pallas_call(kernel, out_shape=(jax.ShapeDtypeStruct((rows, D), BF16),...]
where the time goes in v4:
time: 118 us; the launch traced here: 117 us
  Pallas kernels  116 us (98%)
    pallas_call x1, Pallas kernels, call_kernel(): pl.pallas_call(kernel, out_shape=(jax.ShapeDtypeStruct((rows, D), BF16),...  110 us
    pallas_call x1, Pallas kernels, body(): pl.pallas_call(unpack_kernel, out_shape=tuple((jax.ShapeDtypeStruct(a.sha...  5.87 us

profile of v4, /device:TPU:0, one launch (start us, length us, event | category | flops | bytes accessed | tf_op | source)
XLA Modules:
  0.0 117.1 jit_solution(9978534659973898333)
XLA Ops:
  0.6 110.4 %shard_map.186 = (bf16[1024,768]{1,0:T(8,128)(2,1)}, f32[1024,768]{1,0:T(8,128)}, f32[96,768]{1,0:T(8,128)}, f32[96,768]{1,0:T(8,128)}, f32[96,768]{1,0:T(8,128)}, /*index=5*/f32[8,768]{1,0:T(8,128)}) custom-call(bf16[1024,768]{1,0:T(8,128)(2,1)} %refs_0_.1, bf16[1024,768]{1,0:T(8,128)(2,1)} %refs_1_.1, bf16[3,96,192]{2,1,0:T(8,128)(2,1)} %refs_2_.1, ...), custom_call_target="tpu_custom_call" | custom-call | tf_op jit(solution)/shard_map/pallas_call | solution.py:705
  111.0 5.9 %shard_map.187 = (bf16[1024,768]{1,0:T(8,128)(2,1)}, f32[1024,768]{1,0:T(8,128)}, f32[3,96,192]{2,1,0:T(8,128)}, f32[192,96]{1,0:T(8,128)}, f32[96,768]{1,0:T(8,...) custom-call(bf16[1024,768]{1,0:T(8,128)(2,1)} %get-tuple-element.26.m, ...), custom_call_target="tpu_custom_call" | custom-call | tf_op jit(solution)/shard_map/pallas_call | solution.py:796

commit v5 on v4

--- a/solution.py
+++ b/solution.py
@@ -396,7 +396,8 @@
     zpf = lax.rem(zp + 2, 4)
 
     def zred(m, q, k):
-        src, to = ((zp, zp), (zpf, zp), (zf, zf))[k]
+        ahead = lax.rem(z + k + 1, 4)
+        src, to = ((zp, zp), (zpf, zp), (zf, zf))[k] if m < 2 else (ahead, ahead)
         return remote(
             hs.at[m, src, :, cut(q)], rz.at[m, k, :, cut(q)],
             rzs.at[m, q, k], rzr.at[m, q, k], 2 * to + x, t,
@@ -416,18 +417,21 @@
     def reduce_mid(m, q):
         if not inner:
             return
-        for k, zd in ((1, zpf), (0, zp), (2, zf), (3, z)):
+        places = ((1, zpf), (0, zp), (2, zf), (3, z))
+        if m == 2:
+            places = tuple((k, lax.rem(z + k + 1, 4)) for k in (1, 0, 2, 3))
+        for k, zd in places:
             xred(m, q, zd).wait_recv()
             both = gr[m, 2 * zd + x, :, cut(q)].astype(F32) + rx[m, zd, :, cut(q)].astype(F32)
             if k < 3:
                 hs[m, zd, :, cut(q)] = both.astype(BF16)
             else:
                 outs[m][:, cut(q)] = both
-            if k < 2:
+            if k < (2 if m < 2 else 3):
                 launch(zred(m, q, k))
 
     def reduce_far(m, q):
-        if not inner:
+        if not inner or m == 2:
             return
         zred(m, q, 1).wait_recv()
         far = hs[m, zf, :, cut(q)].astype(F32) + rz[m, 1, :, cut(q)].astype(F32)
@@ -439,9 +443,9 @@
             outs[m][...] = gr[m]
             return
         for q in range(2):
-            zred(m, q, 0).wait_recv()
-            zred(m, q, 2).wait_recv()
-            outs[m][:, cut(q)] += rz[m, 0, :, cut(q)].astype(F32) + rz[m, 2, :, cut(q)].astype(F32)
+            for k in (0, 2) if m < 2 else (0, 1, 2):
+                zred(m, q, k).wait_recv()
+                outs[m][:, cut(q)] += rz[m, k, :, cut(q)].astype(F32)
 
     def down_grad(cols):
         return mm(cot[:, cols], act[...], 0, 0)
@@ -535,10 +539,10 @@
     step(3, 3)
     if inner:
         gather_x(1)
+    step(1, 1)
     add_parameters()
     cp_tok.wait()
     first_norm(0)
-    step(1, 1)
     if inner:
         gather_z(2)
     for b in range(1, nb):
@@ -745,8 +749,8 @@
     d = lax.axis_index("dp")
     moves = []
     for src, via, dst in ((tok_h, tok_v, tok_o), (mix_h, mix_v, mix_o)):
-        for k in range(4):
-            rows = slice(k * src.shape[0] // 4, (k + 1) * src.shape[0] // 4)
+        for k in range(2):
+            rows = slice(k * src.shape[0] // 2, (k + 1) * src.shape[0] // 2)
             sems = sem.at[len(moves)]
             load = pltpu.make_async_copy(src.at[rows], via.at[rows], sems)
             load.start()

time: 118 us -> 117 us (level)
  no operation moved by 1% of the time
where the time goes in v5:
time: 117 us
  Pallas kernels  116 us (99%)
    pallas_call x1, Pallas kernels, call_kernel(): pl.pallas_call(kernel, out_shape=(jax.ShapeDtypeStruct((rows, D), BF16),...  110 us
    pallas_call x1, Pallas kernels, body(): pl.pallas_call(unpack_kernel, out_shape=tuple((jax.ShapeDtypeStruct(a.sha...  5.75 us

profile of v5, /device:TPU:0, one launch (start us, length us, event | category | flops | bytes accessed | tf_op | source)
XLA Modules:
  0.0 116.6 jit_solution(3091445455080151355)
XLA Ops:
  0.6 110.0 %shard_map.186 = (bf16[1024,768]{1,0:T(8,128)(2,1)}, f32[1024,768]{1,0:T(8,128)}, f32[96,768]{1,0:T(8,128)}, f32[96,768]{1,0:T(8,128)}, f32[96,768]{1,0:T(8,128)}, /*index=5*/f32[8,768]{1,0:T(8,128)}) custom-call(bf16[1024,768]{1,0:T(8,128)(2,1)} %refs_0_.1, bf16[1024,768]{1,0:T(8,128)(2,1)} %refs_1_.1, bf16[3,96,192]{2,1,0:T(8,128)(2,1)} %refs_2_.1, ...), custom_call_target="tpu_custom_call" | custom-call | tf_op jit(solution)/shard_map/pallas_call | solution.py:709
  110.7 5.7 %shard_map.187 = (bf16[1024,768]{1,0:T(8,128)(2,1)}, f32[1024,768]{1,0:T(8,128)}, f32[3,96,192]{2,1,0:T(8,128)}, f32[192,96]{1,0:T(8,128)}, f32[96,768]{1,0:T(8,...) custom-call(bf16[1024,768]{1,0:T(8,128)(2,1)} %get-tuple-element.26.m, ...), custom_call_target="tpu_custom_call" | custom-call | tf_op jit(solution)/shard_map/pallas_call | solution.py:800

commit v6 on v5

--- a/solution.py
+++ b/solution.py
@@ -595,7 +595,6 @@
         if b == nb - 1:
             weight_grad(0, in_grad)
             reduce_start(0, 1)
-            reduce_start(0, 0)
             for q in range(2):
                 reduce_far(2, q)
         in_part(b)
@@ -606,6 +605,7 @@
         if b == 0:
             for q in range(2):
                 reduce_mid(2, q)
+    reduce_start(0, 0)
     for b in range(1, nb):
         sum_mid(1, b)
     for q in range(2):
@@ -616,11 +616,11 @@
         reduce_far(1, q)
     small_step(2)
     reduce_mid(0, 1)
+    reduce_far(0, 1)
     reduce_mid(0, 0)
+    reduce_far(0, 0)
     for b in range(1, nb):
         finish_tokens(b)
-    reduce_far(0, 1)
-    reduce_far(0, 0)
     small_step(3)
     reduce_end(2)
     reduce_end(1)

time: 117 us -> 117 us (level)
  no operation moved by 1% of the time
where the time goes in v6:
time: 117 us
  Pallas kernels  116 us (99%)
    pallas_call x1, Pallas kernels, call_kernel(): pl.pallas_call(kernel, out_shape=(jax.ShapeDtypeStruct((rows, D), BF16),...  110 us
    pallas_call x1, Pallas kernels, body(): pl.pallas_call(unpack_kernel, out_shape=tuple((jax.ShapeDtypeStruct(a.sha...  5.75 us

profile of v6, /device:TPU:0, one launch (start us, length us, event | category | flops | bytes accessed | tf_op | source)
XLA Modules:
  0.0 116.6 jit_solution(4641513735781219375)
XLA Ops:
  0.6 110.0 %shard_map.186 = (bf16[1024,768]{1,0:T(8,128)(2,1)}, f32[1024,768]{1,0:T(8,128)}, f32[96,768]{1,0:T(8,128)}, f32[96,768]{1,0:T(8,128)}, f32[96,768]{1,0:T(8,128)}, /*index=5*/f32[8,768]{1,0:T(8,128)}) custom-call(bf16[1024,768]{1,0:T(8,128)(2,1)} %refs_0_.1, bf16[1024,768]{1,0:T(8,128)(2,1)} %refs_1_.1, bf16[3,96,192]{2,1,0:T(8,128)(2,1)} %refs_2_.1, ...), custom_call_target="tpu_custom_call" | custom-call | tf_op jit(solution)/shard_map/pallas_call | solution.py:709
  110.7 5.7 %shard_map.187 = (bf16[1024,768]{1,0:T(8,128)(2,1)}, f32[1024,768]{1,0:T(8,128)}, f32[3,96,192]{2,1,0:T(8,128)}, f32[192,96]{1,0:T(8,128)}, f32[96,768]{1,0:T(8,...) custom-call(bf16[1024,768]{1,0:T(8,128)(2,1)} %get-tuple-element.26.m, ...), custom_call_target="tpu_custom_call" | custom-call | tf_op jit(solution)/shard_map/pallas_call | solution.py:800
